TPU v7x, 32 devices: a whole 2x2x4 slice. The times are simulated.
32 devices in a mesh: blk: 8 (over z, y), group: 4 (over x, core).
Axes of the slice: x: 2, y: 2, z: 4, core: 2. Of those that a mesh axis runs over, the one named last changes fastest.
Arguments:
- vertex_matrix: bfloat16 [32, 1152, 1152], P(('blk', 'group')), may hold values from -0.1875 to 0.1875
- vertex_site: int32 [32, 1152], P(('blk', 'group')), may hold values from 0 to 15
- vertex_time: int32 [32, 1152], P(('blk', 'group')), may hold values from 0 to 1023
- vertex_spin: int32 [32, 1152], P(('blk', 'group')), may hold values from 0 to 1
- free_green: float32 [2, 128], replicated, may hold values from -3 to 3
- plus_table: int32 [32, 128], replicated, may hold values from 0 to 127, each once within a row
- cross_table: int32 [128, 32], P('blk'), may hold values from 0 to 31, each once within a row
Outputs:
- crossed: float32 [2, 128, 32, 128], P(None, 'blk', None, 'group')
Inputs may be any that keep to these rules, and one draw needn't show every extreme that they name: `plus_table`: each row is a permutation of 0 to 127. `cross_table`: each row is a permutation of 0 to 31.
All inputs are finite; a program needn't handle non-finite values.
Results may differ from a plain program's by a relative error of at most 0.0078.
Values may be sent and summed in bfloat16 or wider, within the bound.
A program may use at most 64 MiB of HBM per device.

v0:
```python
import math

import jax
import jax.numpy as jnp
from jax import lax
from jax.sharding import PartitionSpec as P

LX = 4
NW = 8
W = 128
NV = 1152
NT = 1024


def phases(site_ids, time_ids):
    points = jnp.arange(W, dtype=jnp.int32)
    moment = points // NW
    freq_index = points % NW
    kx_part = moment % LX
    ky_part = moment // LX
    rx_part = site_ids % LX
    ry_part = site_ids // LX
    winding = (2 * freq_index + 1)[:, None] * time_ids[None, :] + 2 * NT // LX * (
        kx_part[:, None] * rx_part[None, :] + ky_part[:, None] * ry_part[None, :]
    )
    winding = winding % (2 * NT)
    return winding.astype(jnp.float32) * (math.pi / NT)


def green_pair(matrix, site_ids, time_ids, spin_ids, free_green):
    angles = phases(site_ids, time_ids)
    cosine = jnp.cos(angles)
    sine_part = jnp.sin(angles)
    spin_up = (spin_ids == 0).astype(jnp.float32)[None, :]
    spin_down = (spin_ids == 1).astype(jnp.float32)[None, :]
    fourier_rows = jnp.concatenate(
        [cosine * spin_up, sine_part * spin_up, cosine * spin_down, sine_part * spin_down], 0
    ).astype(jnp.bfloat16)
    projected = jnp.dot(fourier_rows, matrix, preferred_element_type=jnp.float32).astype(
        jnp.bfloat16
    )
    norm_factor = 1.0 / math.sqrt(NV)
    real_free = free_green[0]
    imag_free = free_green[1]
    greens = []
    for spin_index in range(2):
        offset = 2 * W * spin_index
        cosine_rows = fourier_rows[offset : offset + W]
        sine_rows = fourier_rows[offset + W : offset + 2 * W]
        proj_real = projected[offset : offset + W]
        proj_imag = projected[offset + W : offset + 2 * W]
        left_block = jnp.concatenate(
            [
                jnp.concatenate([proj_real, proj_imag], 1),
                jnp.concatenate([proj_imag, -proj_real], 1),
            ],
            0,
        )
        right_block = jnp.concatenate([cosine_rows, sine_rows], 1)
        kernel = lax.dot_general(
            left_block, right_block, (((1,), (1,)), ((), ())), preferred_element_type=jnp.float32
        )
        kernel_real = kernel[:W]
        kernel_imag = kernel[W:]
        half_real = real_free[:, None] * kernel_real - imag_free[:, None] * kernel_imag
        half_imag = real_free[:, None] * kernel_imag + imag_free[:, None] * kernel_real
        green_real = (
            -(half_real * real_free[None, :] - half_imag * imag_free[None, :]) * norm_factor
        )
        green_imag = (
            -(half_real * imag_free[None, :] + half_imag * real_free[None, :]) * norm_factor
        )
        greens.append(jnp.stack([green_real, green_imag], 0))
    green_sum = (greens[0] + greens[1]).astype(jnp.bfloat16)
    return (green_sum, greens[0].astype(jnp.bfloat16), greens[1].astype(jnp.bfloat16))


def direct_terms(sums_piece, perm_row):
    column_ids = jnp.arange(sums_piece.shape[-1], dtype=jnp.int32)
    selector = (perm_row[:, None] == column_ids[None, :]).astype(jnp.bfloat16)
    halfway = jnp.einsum(
        "aj,kcbj->kcab", selector, sums_piece, preferred_element_type=jnp.float32
    ).astype(jnp.bfloat16)
    partner = jnp.einsum("kcaj,bj->kcab", halfway, selector, preferred_element_type=jnp.float32)
    local_copy = sums_piece.astype(jnp.float32)
    real_part = jnp.sum(local_copy[:, 0] * partner[:, 0] - local_copy[:, 1] * partner[:, 1], axis=0)
    imag_part = jnp.sum(local_copy[:, 0] * partner[:, 1] + local_copy[:, 1] * partner[:, 0], axis=0)
    return jnp.stack([real_part, imag_part], 0)


def copy_exchange(up_piece, down_piece, perm_row):
    column_ids = jnp.arange(up_piece.shape[-1], dtype=jnp.int32)
    spin_pieces = jnp.concatenate([up_piece, down_piece], 0)
    lead_values = spin_pieces[:, :, column_ids, perm_row]
    trail_values = spin_pieces[:, :, perm_row, column_ids]
    real_part = jnp.einsum(
        "ka,kb->ab", lead_values[:, 0], trail_values[:, 0], preferred_element_type=jnp.float32
    ) - jnp.einsum(
        "ka,kb->ab", lead_values[:, 1], trail_values[:, 1], preferred_element_type=jnp.float32
    )
    imag_part = jnp.einsum(
        "ka,kb->ab", lead_values[:, 0], trail_values[:, 1], preferred_element_type=jnp.float32
    ) + jnp.einsum(
        "ka,kb->ab", lead_values[:, 1], trail_values[:, 0], preferred_element_type=jnp.float32
    )
    return jnp.stack([real_part, imag_part], 0)


def body(vertex_matrix, vertex_site, vertex_time, vertex_spin, free_green, plus_table, cross_table):
    green_sum, green_up, green_down = green_pair(
        vertex_matrix[0], vertex_site[0], vertex_time[0], vertex_spin[0], free_green
    )
    slices = plus_table.shape[0] // lax.axis_size("blk")
    owned_perms = lax.dynamic_slice_in_dim(plus_table, lax.axis_index("blk") * slices, slices, 0)
    sums_piece = lax.all_gather(green_sum[None], "blk", axis=0, tiled=True)
    up_piece = lax.all_gather(green_up[None], "blk", axis=0, tiled=True)
    down_piece = lax.all_gather(green_down[None], "blk", axis=0, tiled=True)

    def one_slice(perm_row):
        return direct_terms(sums_piece, perm_row) - copy_exchange(up_piece, down_piece, perm_row)

    transfer = jnp.swapaxes(lax.map(one_slice, owned_perms), 0, 1)
    shares = lax.psum_scatter(transfer, "group", scatter_dimension=3, tiled=True)
    regrouped = lax.all_to_all(shares, "blk", split_axis=2, concat_axis=1, tiled=True)
    row_ids = jnp.arange(regrouped.shape[2], dtype=jnp.int32)
    return regrouped[:, cross_table, row_ids[:, None], :]


def solution(mesh):
    in_specs = (
        P(("blk", "group"), None, None),
        P(("blk", "group"), None),
        P(("blk", "group"), None),
        P(("blk", "group"), None),
        P(),
        P(),
        P("blk", None),
    )
    out_specs = P(None, "blk", None, "group")
    return jax.shard_map(body, mesh=mesh, in_specs=in_specs, out_specs=out_specs, check_vma=False)
```

profile of v0, /device:TPU:0, one launch (start us, length us, event | category | flops | bytes accessed | tf_op | source)
XLA Modules:
  0.0 268.0 jit_solution(7998283296705170202)
XLA Ops:
  6.6 0.9 slice_bitcast_fusion.1
  7.4 0.7 fusion.63
  8.1 0.7 fusion.62
  8.9 0.7 reduce.2
  9.6 2.8 %multiply_convert_fusion.3 = (bf16[128,1152]{1,0:T(8,128)(2,1)S(1)}, bf16[128,1152]{1,0:T(8,128)(2,1)S(1)}, bf16[128,1152]{1,0:T(8,128)(2,1)S(1)}, bf16[128,1152]{1,0:T(8,128)(2,1)S(1)}) fusion(f32[1152]{0:T(1024)S(1)} %get-tuple-element.92, s32[1152]{0:T(1024)S(1)} %get-tuple-element.95, s32[128]{0:T(128)S(1)} %get-tuple-element.132, ...), kind=kLoop, calls=%fused_computation.74 | loop fusion | flops 3981312 | bytes 1204224 | tf_op jit(solution)/shard_map/slice | solution.py:48
  12.4 1.9 convolution_convert_fusion.1
  15.6 33.0 %all_gather.9 = bf16[8,2,128,128]{3,2,1,0:T(8,128)(2,1)S(1)} all-gather(bf16[1,2,128,128]{3,2,1,0:T(8,128)(2,1)S(1)} %add_convert_fusion), channel_id=1, replica_groups=mesh['blk'=8,'group'=4] {'blk'}, dimensions={0}, use_global_device_ids=true | all-gather | bytes 589824 | tf_op jit(solution)/shard_map/all_gather | solution.py:115
  48.6 31.5 %all_gather.11 = bf16[8,2,128,128]{3,2,1,0:T(8,128)(2,1)S(1)} all-gather(bf16[1,2,128,128]{3,2,1,0:T(8,128)(2,1)S(1)} %fusion.56), channel_id=1, replica_groups=mesh['blk'=8,'group'=4] {'blk'}, dimensions={0}, use_global_device_ids=true | all-gather | bytes 589824 | tf_op jit(solution)/shard_map/all_gather | solution.py:117
  80.1 31.2 %all_gather.10 = bf16[8,2,128,128]{3,2,1,0:T(8,128)(2,1)S(1)} all-gather(bf16[1,2,128,128]{3,2,1,0:T(8,128)(2,1)S(1)} %fusion.57), channel_id=1, replica_groups=mesh['blk'=8,'group'=4] {'blk'}, dimensions={0}, use_global_device_ids=true | all-gather | bytes 589824 | tf_op jit(solution)/shard_map/all_gather | solution.py:116
  111.2 1.2 pad_maximum_fusion
  112.4 12.9 %copy.28 = bf16[16,2,128,128]{0,1,3,2:T(2,128)(2,1)} copy(bf16[16,2,128,128]{3,2,1,0:T(8,128)(2,1)} %pad_maximum_fusion) | data formatting | bytes 2097152 | tf_op jit(solution)/shard_map/while | solution.py:122
  126.0 76.3 %while.12 = (s32[]{:T(128)}, f32[4,2,128,128]{2,0,1,3:T(4,128)}, bf16[8,2,128,128]{3,2,1,0:T(8,128)(2,1)S(1)}, s32[4,128]{1,0:T(4,128)S(1)}, bf16[16,2,128,128]{0,1,3,2:T(2,128)(2,1)}, /*index=5*/s32[]{:T(128)}, s32[]{:T(128)}) while((s32[]{:T(128)}, f32[4,2,128,128]{2,0,1,3:T(4,128)}, bf16[8,2,128,128]{3,2,1,0:T(8,128)(2,1)S(1)}, ...), condition=%wide.region_3.4_spmd, body=%wide.region_0.3_spmd.sunk | while | flops 138020352 | bytes 6821985 | solution.py:122
  126.0 1.6 fusion.107
  127.7 1.4 subtract_reduce_fusion.2
  129.1 4.3 %gather_fusion = bf16[128,16,2]{1,2,0:T(2,128)(2,1)S(1)} fusion(bf16[16,2,128,128]{0,1,3,2:T(2,128)(2,1)} %get-tuple-element.199, s32[128]{0:T(128)S(1)} %or_bitcast_fusion.5), kind=kCustom, calls=%fused_computation.1.clone.1 | custom fusion | bytes 17408 | tf_op jit(solution)/shard_map/while/body/eval_jaxpr/gather | solution.py:95
  133.6 4.3 %gather_fusion.1 = bf16[128,16,2]{1,2,0:T(2,128)(2,1)S(1)} fusion(bf16[16,2,128,128]{0,1,3,2:T(2,128)(2,1)} %get-tuple-element.199, s32[128]{0:T(128)S(1)} %get-tuple-element.177), kind=kCustom, calls=%fused_computation.clone.1 | custom fusion | bytes 17408 | tf_op jit(solution)/shard_map/while/body/eval_jaxpr/gather | solution.py:94
  137.9 0.7 fusion.109
  138.6 0.9 copy.46
  140.6 4.5 %dynamic_update_slice.7 = f32[4,2,128,128]{2,0,1,3:T(4,128)} dynamic-update-slice(f32[4,2,128,128]{2,0,1,3:T(4,128)} %get-tuple-element.189, f32[1,2,128,128]{2,0,1,3:T(1,128)S(1)} %copy.49, s32[]{:T(128)S(6)} %copy.53, s32[]{:T(128)} %constant.118.clone.1..sunk, s32[]{:T(128)} %constant.118.clone.1..sunk, s32[]{:T(128)} %constant.118.clone.1..sunk) | dynamic-update-slice | bytes 262148 | tf_op jit(solution)/shard_map/while/body/jit(dynamic_update_index_in_dim)/dynamic_update_slice | solution.py:122
  145.1 1.6 fusion.107
  146.8 1.4 subtract_reduce_fusion.2
  148.2 4.3 %gather_fusion = bf16[128,16,2]{1,2,0:T(2,128)(2,1)S(1)} fusion(bf16[16,2,128,128]{0,1,3,2:T(2,128)(2,1)} %get-tuple-element.199, s32[128]{0:T(128)S(1)} %or_bitcast_fusion.5), kind=kCustom, calls=%fused_computation.1.clone.1 | custom fusion | bytes 17408 | tf_op jit(solution)/shard_map/while/body/eval_jaxpr/gather | solution.py:95
  152.6 4.3 %gather_fusion.1 = bf16[128,16,2]{1,2,0:T(2,128)(2,1)S(1)} fusion(bf16[16,2,128,128]{0,1,3,2:T(2,128)(2,1)} %get-tuple-element.199, s32[128]{0:T(128)S(1)} %get-tuple-element.177), kind=kCustom, calls=%fused_computation.clone.1 | custom fusion | bytes 17408 | tf_op jit(solution)/shard_map/while/body/eval_jaxpr/gather | solution.py:94
  156.9 0.7 fusion.109
  157.6 0.9 copy.46
  159.6 4.5 %dynamic_update_slice.7 = f32[4,2,128,128]{2,0,1,3:T(4,128)} dynamic-update-slice(f32[4,2,128,128]{2,0,1,3:T(4,128)} %get-tuple-element.189, f32[1,2,128,128]{2,0,1,3:T(1,128)S(1)} %copy.49, s32[]{:T(128)S(6)} %copy.53, s32[]{:T(128)} %constant.118.clone.1..sunk, s32[]{:T(128)} %constant.118.clone.1..sunk, s32[]{:T(128)} %constant.118.clone.1..sunk) | dynamic-update-slice | bytes 262148 | tf_op jit(solution)/shard_map/while/body/jit(dynamic_update_index_in_dim)/dynamic_update_slice | solution.py:122
  164.1 1.6 fusion.107
  165.9 1.4 subtract_reduce_fusion.2
  167.3 4.3 %gather_fusion = bf16[128,16,2]{1,2,0:T(2,128)(2,1)S(1)} fusion(bf16[16,2,128,128]{0,1,3,2:T(2,128)(2,1)} %get-tuple-element.199, s32[128]{0:T(128)S(1)} %or_bitcast_fusion.5), kind=kCustom, calls=%fused_computation.1.clone.1 | custom fusion | bytes 17408 | tf_op jit(solution)/shard_map/while/body/eval_jaxpr/gather | solution.py:95
  171.7 4.3 %gather_fusion.1 = bf16[128,16,2]{1,2,0:T(2,128)(2,1)S(1)} fusion(bf16[16,2,128,128]{0,1,3,2:T(2,128)(2,1)} %get-tuple-element.199, s32[128]{0:T(128)S(1)} %get-tuple-element.177), kind=kCustom, calls=%fused_computation.clone.1 | custom fusion | bytes 17408 | tf_op jit(solution)/shard_map/while/body/eval_jaxpr/gather | solution.py:94
  176.0 0.7 fusion.109
  176.7 0.9 copy.46
  178.7 4.5 %dynamic_update_slice.7 = f32[4,2,128,128]{2,0,1,3:T(4,128)} dynamic-update-slice(f32[4,2,128,128]{2,0,1,3:T(4,128)} %get-tuple-element.189, f32[1,2,128,128]{2,0,1,3:T(1,128)S(1)} %copy.49, s32[]{:T(128)S(6)} %copy.53, s32[]{:T(128)} %constant.118.clone.1..sunk, s32[]{:T(128)} %constant.118.clone.1..sunk, s32[]{:T(128)} %constant.118.clone.1..sunk) | dynamic-update-slice | bytes 262148 | tf_op jit(solution)/shard_map/while/body/jit(dynamic_update_index_in_dim)/dynamic_update_slice | solution.py:122
  183.2 1.6 fusion.107
  184.9 1.4 subtract_reduce_fusion.2
  186.3 4.3 %gather_fusion = bf16[128,16,2]{1,2,0:T(2,128)(2,1)S(1)} fusion(bf16[16,2,128,128]{0,1,3,2:T(2,128)(2,1)} %get-tuple-element.199, s32[128]{0:T(128)S(1)} %or_bitcast_fusion.5), kind=kCustom, calls=%fused_computation.1.clone.1 | custom fusion | bytes 17408 | tf_op jit(solution)/shard_map/while/body/eval_jaxpr/gather | solution.py:95
  190.8 4.3 %gather_fusion.1 = bf16[128,16,2]{1,2,0:T(2,128)(2,1)S(1)} fusion(bf16[16,2,128,128]{0,1,3,2:T(2,128)(2,1)} %get-tuple-element.199, s32[128]{0:T(128)S(1)} %get-tuple-element.177), kind=kCustom, calls=%fused_computation.clone.1 | custom fusion | bytes 17408 | tf_op jit(solution)/shard_map/while/body/eval_jaxpr/gather | solution.py:94
  195.0 0.7 fusion.109
  195.8 0.9 copy.46
  197.8 4.5 %dynamic_update_slice.7 = f32[4,2,128,128]{2,0,1,3:T(4,128)} dynamic-update-slice(f32[4,2,128,128]{2,0,1,3:T(4,128)} %get-tuple-element.189, f32[1,2,128,128]{2,0,1,3:T(1,128)S(1)} %copy.49, s32[]{:T(128)S(6)} %copy.53, s32[]{:T(128)} %constant.118.clone.1..sunk, s32[]{:T(128)} %constant.118.clone.1..sunk, s32[]{:T(128)} %constant.118.clone.1..sunk) | dynamic-update-slice | bytes 262148 | tf_op jit(solution)/shard_map/while/body/jit(dynamic_update_index_in_dim)/dynamic_update_slice | solution.py:122
  203.7 33.4 %all-reduce.3.cloned.1.call-done = f32[2,4,128,128]{2,1,0,3:T(4,128)} async-done(((f32[2,4,128,128]{2,1,0,3:T(4,128)}), f32[2,4,128,128]{2,1,0,3:T(4,128)}) %all-reduce.3.cloned.1.call-update) | async-done | bytes 524304
  237.1 0.9 constant_dynamic-slice_fusion.1
  238.3 1.0 reshape.319
  239.3 5.5 %all-to-all-start = ((f32[8,1,4096]{2,1,0:T(1,128)}), f32[8,1,4096]{2,1,0:T(1,128)S(1)}, u32[]{:S(2)}, u32[]{:S(2)}) async-start(f32[8,1,4096]{2,1,0:T(1,128)} %reshape.319), calls=%async_computation | async-start | bytes 262144 | tf_op jit(solution)/shard_map/all_to_all | solution.py:124
  244.9 7.2 %all-to-all-done = f32[8,1,4096]{2,1,0:T(1,128)S(1)} async-done(((f32[8,1,4096]{2,1,0:T(1,128)}), f32[8,1,4096]{2,1,0:T(1,128)S(1)}, u32[]{:S(2)}, u32[]{:S(2)}) %all-to-all-start) | async-done | bytes 131104 | tf_op jit(solution)/shard_map/all_to_all | solution.py:124
  252.6 1.0 reduce.11
  254.4 4.8 %gather_fusion.2 = f32[512,2,32]{2,1,0:T(2,128)} fusion(f32[2,32,16,32]{3,0,2,1:T(2,128)S(1)} %copy.33, s32[512]{0:T(512)S(1)} %reshape.301), kind=kCustom, calls=%fused_computation.2 | custom fusion | bytes 266240 | tf_op jit(solution)/shard_map/gather | solution.py:126
  259.2 1.9 copy.39
  (84 shorter events, 9.7 us)
Async XLA Ops:
  6.5 5.9 %copy-start = (bf16[1,1152,1152]{2,1,0:T(8,128)(2,1)S(1)}, bf16[1,1152,1152]{2,1,0:T(8,128)(2,1)}, u32[]{:S(2)}) copy-start(bf16[1,1152,1152]{2,1,0:T(8,128)(2,1)} %param.9) | copy-start | bytes 7962628
  6.5 230.5 %all-reduce.3.cloned.1.call-start = ((), (), s32[]{:S(2)}) async-start(), calls=%async_computation.1 | async-start | bytes 1048576
  126.0 76.3 %copy-start.2 = (u32[32]{0:T(128)S(1)}, u32[32]{0:T(128)}, u32[]{:S(2)}) copy-start(u32[32]{0:T(128)} %constant.180) | copy-start | bytes 388
  202.3 42.5 %copy-start.1 = (s32[16,32]{1,0:T(8,128)S(1)}, s32[16,32]{1,0:T(8,128)}, u32[]{:S(2)}) copy-start(s32[16,32]{1,0:T(8,128)} %param.15) | copy-start | bytes 6148
  239.3 12.9 %all-to-all-start = ((f32[8,1,4096]{2,1,0:T(1,128)}), f32[8,1,4096]{2,1,0:T(1,128)S(1)}, u32[]{:S(2)}, u32[]{:S(2)}) async-start(f32[8,1,4096]{2,1,0:T(1,128)} %reshape.319), calls=%async_computation | async-start | bytes 262144 | tf_op jit(solution)/shard_map/all_to_all | solution.py:124
Sparse Core Ops, SparseCore 0:
  202.4 34.6 all-reduce.2
where the time goes:
time: 270 us; the launch traced here: 268 us
  blocking collectives  95.7 us (35%)
  local copies, waits for them, and re-layouts  85.7 us (32%)
  waiting for transfers between devices  40.7 us (15%)
  between operations  14.3 us (5%)
  other arithmetic  13.5 us (5%)
  matrix products  12.4 us (5%)
  starting transfers between devices  5.52 us (2%)
    unnamed x2, waiting for transfers between devices  33.4 us
    all_gather x1, blocking collectives, body(): sums_piece = lax.all_gather(green_sum[None], 'blk', axis=0, tiled=True)  33 us
    all_gather x1, blocking collectives, body(): down_piece = lax.all_gather(green_down[None], 'blk', axis=0, tiled=True)  31.5 us
    all_gather x1, blocking collectives, body(): up_piece = lax.all_gather(green_up[None], 'blk', axis=0, tiled=True)  31.2 us
    dynamic_update_slice x8, local copies, waits for them, and re-layouts, body(): transfer = jnp.swapaxes(lax.map(one_slice, owned_perms), 0, 1)  18.4 us
    gather x4, local copies, waits for them, and re-layouts, copy_exchange(): lead_values = spin_pieces[:, :, column_ids, perm_row]  17.1 us
    gather x4, local copies, waits for them, and re-layouts, copy_exchange(): trail_values = spin_pieces[:, :, perm_row, column_ids]  17 us
    while x1, local copies, waits for them, and re-layouts, body(): transfer = jnp.swapaxes(lax.map(one_slice, owned_perms), 0, 1)  12.9 us
  transfers between devices with their start and end apart: 2, of which 2 were waited for; matrix products, arithmetic and copies ran while one was open for 0% of the time, Pallas kernels for 0%

commit v1 on v0

--- a/solution.py
+++ b/solution.py
@@ -1,8 +1,11 @@
+import functools
 import math
 
 import jax
 import jax.numpy as jnp
 from jax import lax
+from jax.experimental import pallas as pl
+from jax.experimental.pallas import tpu as pltpu
 from jax.sharding import PartitionSpec as P
 
 LX = 4
@@ -106,7 +109,7 @@
     return jnp.stack([real_part, imag_part], 0)
 
 
-def body(vertex_matrix, vertex_site, vertex_time, vertex_spin, free_green, plus_table, cross_table):
+def plain_body(vertex_matrix, vertex_site, vertex_time, vertex_spin, free_green, plus_table, cross_table):
     green_sum, green_up, green_down = green_pair(
         vertex_matrix[0], vertex_site[0], vertex_time[0], vertex_spin[0], free_green
     )
@@ -124,6 +127,414 @@
     regrouped = lax.all_to_all(shares, "blk", split_axis=2, concat_axis=1, tiled=True)
     row_ids = jnp.arange(regrouped.shape[2], dtype=jnp.int32)
     return regrouped[:, cross_table, row_ids[:, None], :]
+
+
+BF = jnp.bfloat16
+F32 = jnp.float32
+MESH = pl.DeviceIdType.MESH
+INNER = 2
+PARTS = 4
+CHUNKS = 3
+
+
+def iota(shape, dim):
+    return lax.broadcasted_iota(jnp.int32, shape, dim)
+
+
+def one_hot(condition):
+    return jnp.where(condition, 1.0, 0.0).astype(BF)
+
+
+def dot(left, right):
+    return jnp.dot(left, right, preferred_element_type=F32)
+
+
+def dot_nt(left, right):
+    return lax.dot_general(left, right, (((1,), (1,)), ((), ())), preferred_element_type=F32)
+
+
+def kernel(
+    nblk,
+    ngroup,
+    site_ref,
+    time_ref,
+    spin_ref,
+    free_ref,
+    plus_ref,
+    cross_ref,
+    matrix_hbm,
+    out_ref,
+    matrix,
+    rows,
+    kern,
+    st,
+    lr,
+    lr_send,
+    sel_b,
+    sel_a,
+    sel_out,
+    spread,
+    prow,
+    sb,
+    halfway,
+    tsend,
+    trecv,
+    matrix_sem,
+    st_send,
+    st_recv,
+    lr_send_sem,
+    lr_recv,
+    t_send,
+    t_recv,
+):
+    nz = nblk // INNER
+    na = W // nblk
+    nb = W // ngroup
+    nq = plus_ref.shape[0]
+    half = na * nz
+    npair = nq // 2
+    nchunk = W // na
+    nv = site_ref.shape[1]
+    piece = nv // CHUNKS
+    blk = lax.axis_index("blk")
+    grp = lax.axis_index("group")
+    zz = blk // INNER
+    yy = blk % INNER
+    plane = [(dy, dg) for dy in range(INNER) for dg in range(ngroup) if dy + dg > 0]
+
+    def plane_peer(dy, dg):
+        return (zz * INNER + (yy + dy) % INNER, (grp + dg) % ngroup)
+
+    def z_peer(dz):
+        return (((zz + dz) % nz) * INNER + yy, grp)
+
+    barrier = pltpu.get_barrier_semaphore()
+    for dy, dg in plane:
+        pl.semaphore_signal(barrier, inc=1, device_id=plane_peer(dy, dg), device_id_type=MESH)
+    for dz in range(1, nz):
+        pl.semaphore_signal(barrier, inc=1, device_id=z_peer(dz), device_id_type=MESH)
+
+    def matrix_copy(index):
+        cols = pl.ds(pl.multiple_of(index * piece, 128), piece)
+        return pltpu.make_async_copy(
+            matrix_hbm.at[:, cols], matrix.at[:, cols], matrix_sem.at[index]
+        )
+
+    for index in range(CHUNKS):
+        matrix_copy(index).start()
+
+    site = site_ref[...]
+    rx = site % LX
+    ry = site // LX
+    freq = iota((NW, nv), 0)
+    winding = ((2 * freq + 1) * time_ref[...]) % (2 * NT)
+    angles = winding.astype(F32) * (math.pi / NT)
+    cosine = jnp.cos(angles)
+    sine = jnp.sin(angles)
+    spin = jnp.broadcast_to(spin_ref[...], (NW, nv))
+    up = jnp.where(spin == 0, 1.0, 0.0)
+    down = jnp.where(spin == 1, 1.0, 0.0)
+    rx = jnp.broadcast_to(rx, (NW, nv))
+    ry = jnp.broadcast_to(ry, (NW, nv))
+    for first in range(0, W // NW, 2):
+        c_rows = []
+        s_rows = []
+        for k in (first, first + 1):
+            turn = ((k % LX) * rx + (k // LX) * ry) % 4
+            odd = turn % 2 == 1
+            c_sign = jnp.where((turn == 1) | (turn == 2), -1.0, 1.0)
+            s_sign = jnp.where(turn >= 2, -1.0, 1.0)
+            c_rows.append(jnp.where(odd, sine, cosine) * c_sign)
+            s_rows.append(jnp.where(odd, cosine, sine) * s_sign)
+        both_up = jnp.concatenate([up, up], 0)
+        both_down = jnp.concatenate([down, down], 0)
+        c_both = jnp.concatenate(c_rows, 0)
+        s_both = jnp.concatenate(s_rows, 0)
+        at = first * NW
+        rows[pl.ds(at, 2 * NW), :] = (c_both * both_up).astype(BF)
+        rows[pl.ds(W + at, 2 * NW), :] = (s_both * both_up).astype(BF)
+        rows[pl.ds(2 * W + at, 2 * NW), :] = (c_both * both_down).astype(BF)
+        rows[pl.ds(3 * W + at, 2 * NW), :] = (s_both * both_down).astype(BF)
+
+    kern[...] = jnp.zeros_like(kern)
+
+    def project(index, carry):
+        matrix_copy(index).wait()
+        cols = pl.ds(pl.multiple_of(index * piece, 128), piece)
+        projected = dot(rows[...], matrix[:, cols]).astype(BF)
+        for s in range(2):
+            kern[s] += dot_nt(
+                projected[2 * W * s : 2 * W * (s + 1)], rows[pl.ds(2 * W * s, 2 * W), cols]
+            )
+        return carry
+
+    lax.fori_loop(0, CHUNKS, project, 0)
+
+    ga_re = jnp.broadcast_to(free_ref[0:1, :], (W, W))
+    ga_im = jnp.broadcast_to(free_ref[1:2, :], (W, W))
+    gb_re, gb_im = ga_re, ga_im
+    ga_re = ga_re.T
+    ga_im = ga_im.T
+    norm_factor = 1.0 / math.sqrt(NV)
+    greens = []
+    for s in range(2):
+        k_re = kern[s, :W, :W] + kern[s, W:, W:]
+        k_im = kern[s, W:, :W] - kern[s, :W, W:]
+        h_re = ga_re * k_re - ga_im * k_im
+        h_im = ga_re * k_im + ga_im * k_re
+        greens.append(-(h_re * gb_re - h_im * gb_im) * norm_factor)
+        greens.append(-(h_re * gb_im + h_im * gb_re) * norm_factor)
+    turned = [g.T for g in greens]
+    st[0, :W, :] = (turned[0] + turned[2]).astype(BF)
+    st[0, W:, :] = (turned[1] + turned[3]).astype(BF)
+
+    pl.semaphore_wait(barrier, len(plane) + nz - 1)
+
+    def st_copy(slot, dy, dg):
+        return pltpu.make_async_remote_copy(
+            src_ref=st.at[0],
+            dst_ref=st.at[slot],
+            send_sem=st_send.at[slot],
+            recv_sem=st_recv.at[slot],
+            device_id=plane_peer(dy, dg),
+            device_id_type=MESH,
+        )
+
+    def lr_copy(slot, dy, dg):
+        wanted = ((yy + dy) % INNER) * ngroup + (grp + dg) % ngroup
+        return pltpu.make_async_remote_copy(
+            src_ref=lr_send.at[wanted],
+            dst_ref=lr.at[slot],
+            send_sem=lr_send_sem.at[slot],
+            recv_sem=lr_recv.at[slot],
+            device_id=plane_peer(dy, dg),
+            device_id_type=MESH,
+        )
+
+    for slot, (dy, dg) in enumerate(plane):
+        st_copy(slot + 1, dy, dg).start()
+
+    greens = [g.astype(BF).astype(F32) for g in greens]
+    turned = [g.astype(BF).astype(F32) for g in turned]
+    plus = plus_ref[...].astype(F32)
+    plus_turned = jnp.concatenate([plus, jnp.zeros((W - nq, W), F32)], 0).T
+    expand = one_hot(iota((W, W), 1) // PARTS == iota((W, W), 0))
+    index = dot(plus_turned.astype(BF), expand).astype(jnp.int32)
+    lane = iota((W, W), 1)
+    part = lane % PARTS
+
+    def choose(values):
+        picked = values[0]
+        for g in range(1, PARTS):
+            picked = jnp.where(part == g, values[g], picked)
+        return picked
+
+    lead = choose([jnp.take_along_axis(g, index, axis=1) for g in greens])
+    trail = [jnp.take_along_axis(g, index, axis=1) for g in turned]
+    trail_re = choose([trail[0], -trail[1], trail[2], -trail[3]]).T
+    trail_im = choose([trail[1], trail[0], trail[3], trail[2]]).T
+    order = [INNER * z + y for y in range(INNER) for z in range(nz)]
+    lead = jnp.concatenate([lead[na * i : na * (i + 1)] for i in order], 0).T
+
+    def shifted(value, by):
+        by = by % W
+        return value if by == 0 else pltpu.roll(value, by, 1)
+
+    for j in range(ngroup):
+        left = jnp.where(
+            lane < nb, shifted(trail_re, -nb * j), shifted(trail_im, nb - nb * j)
+        )
+        for y in range(INNER):
+            joined = jnp.where(lane < half, left, shifted(lead, half - half * y))
+            lr_send[y * ngroup + j] = joined.astype(BF)
+    for slot, (dy, dg) in enumerate(plane):
+        lr_copy(slot + 1, dy, dg).start()
+    lr[0] = lr_send[yy * ngroup + grp]
+
+    plus_bf = plus.astype(BF)
+    my_b = one_hot(iota((nb, W), 1) == iota((nb, W), 0) + nb * grp)
+    plus_b = dot_nt(my_b, plus_bf).astype(jnp.int32)
+    for q in range(nq):
+        column = jnp.broadcast_to(plus_b[:, q : q + 1], (nb, W))
+        sel_b[pl.ds(q * nb, nb), :] = one_hot(column == iota((nb, W), 1))
+    place = (lane % half) // na * (na * INNER) + na * yy + lane % na
+    my_a = one_hot(iota((W, W), 0) == place)
+    prow[...] = dot(plus_bf, my_a)
+
+    def pair_selector(pair, carry):
+        first = prow[pl.ds(2 * pair, 1), :]
+        second = prow[pl.ds(2 * pair + 1, 1), :]
+        low = lane < half
+        hit = iota((W, W), 0) == jnp.where(
+            low, jnp.broadcast_to(first, (W, W)), jnp.broadcast_to(second, (W, W))
+        ).astype(jnp.int32)
+        sel_a[pair, :W, :] = one_hot(hit & low)
+        sel_a[pair, W:, :] = one_hot(hit & (lane >= half))
+        return carry
+
+    lax.fori_loop(0, npair, pair_selector, 0)
+
+    width = nz * W
+    source = iota((width, W), 0)
+    target = (source // na) % nz * W + source // half * na + source % na
+    for z in range(nz):
+        spread[:, z * W : (z + 1) * W] = one_hot(target == iota((width, W), 1) + z * W)
+
+    same = one_hot(iota((nq, nq), 0) == iota((nq, nq), 1))
+    crossing = dot_nt(same, cross_ref[...].astype(F32).astype(BF)).astype(jnp.int32)
+    for r in range(na):
+        column = jnp.broadcast_to(crossing[:, r : r + 1] * na + r, (nq, nq * na))
+        sel_out[pl.ds(r * nq, nq), :] = one_hot(column == iota((nq, nq * na), 1))
+
+    def first_selection(slot, carry):
+        @pl.when(slot > 0)
+        def _():
+            st_copy(slot, 0, 1).wait_recv()
+
+        for c in range(2):
+            mine = st[slot, pl.ds(pl.multiple_of(c * W + nb * grp, nb), nb), :]
+            sb[slot, c] = dot(mine, my_a)
+            chosen = dot_nt(sel_b[...], st[slot, c * W : (c + 1) * W, :]).astype(BF)
+            for q in range(nq):
+                halfway[q // 2, slot, c, :, pl.ds((q % 2) * W, W)] = chosen[
+                    q * nb : (q + 1) * nb
+                ]
+        return carry
+
+    lax.fori_loop(0, len(plane) + 1, first_selection, 0)
+
+    for slot, (dy, dg) in enumerate(plane):
+        lr_copy(slot + 1, dy, dg).wait_recv()
+
+    nw = len(plane) + 1
+    four = W // (nw * PARTS)
+    depth = four * PARTS
+
+    def t_copy(dz, chunk):
+        cols = pl.ds(pl.multiple_of(chunk * W, W), W)
+        return pltpu.make_async_remote_copy(
+            src_ref=tsend.at[(zz + dz) % nz, :, cols],
+            dst_ref=trecv.at[dz, :, cols],
+            send_sem=t_send.at[dz, chunk],
+            recv_sem=t_recv.at[dz, chunk],
+            device_id=z_peer(dz),
+            device_id_type=MESH,
+        )
+
+    def measure_chunk(chunk, carry):
+        totals = []
+        for sub in range(nz):
+            pair = chunk * nz + sub
+            partner = dot(halfway[pair].reshape(nw * 2 * nb, 2 * W), sel_a[pair])
+            t_re = jnp.zeros((nb, W), F32)
+            t_im = jnp.zeros((nb, W), F32)
+            for w in range(nw):
+                s_re = sb[w, 0]
+                s_im = sb[w, 1]
+                p_re = partner[2 * nb * w : 2 * nb * w + nb]
+                p_im = partner[2 * nb * w + nb : 2 * nb * (w + 1)]
+                t_re = t_re + (s_re * p_re - s_im * p_im)
+                t_im = t_im + (s_re * p_im + s_im * p_re)
+            pairs = four // 2
+            if sub % pairs == 0:
+                start = pl.multiple_of((chunk * (nz // pairs) + sub // pairs) * depth, depth)
+                stacked = lr[:, pl.ds(start, depth), :].reshape(W, W).astype(F32)
+                trailing = stacked.T[:half].astype(BF)
+                leading = jnp.where(lane < half, pltpu.roll(stacked, half, 1), stacked)
+                row_q = iota((W, W), 0) % depth // PARTS
+            masked = jnp.where(row_q == 2 * (sub % pairs) + lane // half, leading, 0.0)
+            exchange = dot(trailing, masked.astype(BF))
+            totals.append((jnp.concatenate([t_re, t_im], 0) - exchange).astype(BF))
+        moved = dot(jnp.concatenate(totals, 1), spread[...]).astype(BF)
+        cols = pl.ds(pl.multiple_of(chunk * W, W), W)
+        for z in range(nz):
+            tsend[z, :, cols] = moved[:, z * W : (z + 1) * W]
+        for dz in range(1, nz):
+            t_copy(dz, chunk).start()
+        return carry
+
+    chunks = nq // nchunk
+    lax.fori_loop(0, chunks, measure_chunk, 0)
+
+    out_ref[...] = dot_nt(sel_out[...], tsend[zz])
+    for dz in range(1, nz):
+        for chunk in range(chunks):
+            t_copy(dz, chunk).wait_recv()
+        out_ref[...] += dot_nt(sel_out[...], trecv[dz])
+
+    for slot, (dy, dg) in enumerate(plane):
+        st_copy(slot + 1, dy, dg).wait_send()
+        lr_copy(slot + 1, dy, dg).wait_send()
+    for dz in range(1, nz):
+        for chunk in range(chunks):
+            t_copy(dz, chunk).wait_send()
+
+
+def kernel_body(
+    vertex_matrix, vertex_site, vertex_time, vertex_spin, free_green, plus_table, cross_table
+):
+    nblk = lax.axis_size("blk")
+    ngroup = lax.axis_size("group")
+    nv = vertex_matrix.shape[-1]
+    nq = plus_table.shape[0]
+    nz = nblk // INNER
+    na = W // nblk
+    nb = W // ngroup
+    nw = INNER * ngroup
+    npair = nq // 2
+    chunks = nq // (W // na)
+    vmem = pl.BlockSpec(memory_space=pltpu.VMEM)
+    dma = pltpu.SemaphoreType.DMA
+    out = pl.pallas_call(
+        functools.partial(kernel, nblk, ngroup),
+        out_shape=jax.ShapeDtypeStruct((na * nq, 2 * nb), F32),
+        in_specs=[vmem] * 6 + [pl.BlockSpec(memory_space=pl.ANY)],
+        out_specs=vmem,
+        scratch_shapes=[
+            pltpu.VMEM((nv, nv), BF),
+            pltpu.VMEM((4 * W, nv), BF),
+            pltpu.VMEM((2, 2 * W, 2 * W), F32),
+            pltpu.VMEM((nw, 2 * W, W), BF),
+            pltpu.VMEM((nw, W, W), BF),
+            pltpu.VMEM((nw, W, W), BF),
+            pltpu.VMEM((nq * nb, W), BF),
+            pltpu.VMEM((npair, 2 * W, W), BF),
+            pltpu.VMEM((na * nq, nq * na), BF),
+            pltpu.VMEM((nz * W, nz * W), BF),
+            pltpu.VMEM((nq, W), F32),
+            pltpu.VMEM((nw, 2, nb, W), F32),
+            pltpu.VMEM((npair, nw, 2, nb, 2 * W), BF),
+            pltpu.VMEM((nz, 2 * nb, nq * na), BF),
+            pltpu.VMEM((nz, 2 * nb, nq * na), BF),
+            dma((CHUNKS,)),
+            dma((nw,)),
+            dma((nw,)),
+            dma((nw,)),
+            dma((nw,)),
+            dma((nz, chunks)),
+            dma((nz, chunks)),
+        ],
+        compiler_params=pltpu.CompilerParams(
+            collective_id=0, has_side_effects=True, vmem_limit_bytes=40 * 1024 * 1024
+        ),
+    )(
+        vertex_site,
+        vertex_time,
+        vertex_spin,
+        free_green,
+        plus_table,
+        cross_table,
+        vertex_matrix[0],
+    )
+    return out.reshape(na, nq, 2, nb).transpose(2, 0, 1, 3)
+
+
+def fits(mesh):
+    nblk, ngroup = mesh.shape["blk"], mesh.shape["group"]
+    if nblk % INNER or W % nblk or W % ngroup:
+        return False
+    nz, na, nb = nblk // INNER, W // nblk, W // ngroup
+    return nz == 4 and 2 * nz * na == W and 4 * nb == W and na % 16 == 0 and nb % 16 == 0
 
 
 def solution(mesh):
@@ -137,4 +548,10 @@
         P("blk", None),
     )
     out_specs = P(None, "blk", None, "group")
-    return jax.shard_map(body, mesh=mesh, in_specs=in_specs, out_specs=out_specs, check_vma=False)
+
+    def chosen(*args):
+        matrix, plus = args[0], args[5]
+        small = fits(mesh) and PARTS * plus.shape[0] == W and matrix.shape[-1] % (128 * CHUNKS) == 0
+        return (kernel_body if small else plain_body)(*args)
+
+    return jax.shard_map(chosen, mesh=mesh, in_specs=in_specs, out_specs=out_specs, check_vma=False)

time: 270 us -> 36 us (0.13)
  blocking collectives: 95.7 us -> 0 us
  local copies, waits for them, and re-layouts: 85.7 us -> 7.23 us
  waiting for transfers between devices: 40.7 us -> 0 us
  Pallas kernels: 0 us -> 28.3 us
  between operations: 14.3 us -> 0.03 us
  other arithmetic: 13.5 us -> 0 us
  matrix products: 12.4 us -> 0 us
  starting transfers between devices: 5.52 us -> 0 us
    all_gather x3 -> x0, blocking collectives: 95.7 us -> none  [the longest x1 33 us: body(): sums_piece = lax.all_gather(green_sum[None], 'blk', axis=0, tiled=True)]
    gather x10 -> x0, local copies, waits for them, and re-layouts: 40.8 us -> none  [the longest x4 17.1 us: copy_exchange(): lead_values = spin_pieces[:, :, column_ids, perm_row]]
    unnamed x2 -> x0, waiting for transfers between devices: 33.4 us -> none
    pallas_call x0 -> x1, Pallas kernels: none -> 28.3 us  [kernel_body(): pl.pallas_call(functools.partial(kernel, nblk, ngroup), out_shape=jax.Sha...]
    dynamic_update_slice x8 -> x0, local copies, waits for them, and re-layouts: 18.4 us -> none  [body(): transfer = jnp.swapaxes(lax.map(one_slice, owned_perms), 0, 1)]
    while x1 -> x0, local copies, waits for them, and re-layouts: 12.9 us -> none  [body(): transfer = jnp.swapaxes(lax.map(one_slice, owned_perms), 0, 1)]
    dot_general x23 -> x0, matrix products: 12.4 us -> none  [the longest x4 6.48 us: direct_terms(): jnp.einsum('kcaj,bj->kcab', halfway, selector, preferred_element_type=jnp...]
    slice x24 -> x0, local copies, waits for them, and re-layouts: 7.79 us -> none  [the longest x4 3.63 us: copy_exchange(): lead_values[:, 0]]
  transfers between devices with their start and end apart: 2 -> 0, of which waited for: 2 -> 0; matrix products, arithmetic and copies ran while one was open for 0% -> 0% of each run, Pallas kernels for 0% -> 0%
where the time goes in v1:
time: 36 us; the launch traced here: 35.5 us
  Pallas kernels  28.3 us (79%)
  local copies, waits for them, and re-layouts  7.23 us (20%)
    pallas_call x1, Pallas kernels, kernel_body(): pl.pallas_call(functools.partial(kernel, nblk, ngroup), out_shape=jax.Sha...  28.3 us
    unnamed x14, local copies, waits for them, and re-layouts  5.9 us
    transpose x1, local copies, waits for them, and re-layouts, kernel_body(): return out.reshape(na, nq, 2, nb).transpose(2, 0, 1, 3)  1.05 us

profile of v1, /device:TPU:0, one launch (start us, length us, event | category | flops | bytes accessed | tf_op | source)
XLA Modules:
  0.0 35.5 jit_solution(6833096287895846390)
XLA Ops:
  0.0 0.0 copy-start
  0.0 1.7 %copy-done = bf16[1,1152,1152]{2,1,0:T(8,128)(2,1)S(1)} copy-done((bf16[1,1152,1152]{2,1,0:T(8,128)(2,1)S(1)}, bf16[1,1152,1152]{2,1,0:T(8,128)(2,1)}, u32[]{:S(2)}) %copy-start) | copy-done | bytes 2654232
  1.8 0.0 copy-start.1
  1.8 0.7 %copy-done.1 = s32[32,128]{1,0:T(8,128)S(1)} copy-done((s32[32,128]{1,0:T(8,128)S(1)}, s32[32,128]{1,0:T(8,128)}, u32[]{:S(2)}) %copy-start.1) | copy-done | bytes 16408
  2.5 0.0 copy-start.2
  2.5 0.7 %copy-done.2 = s32[16,32]{1,0:T(8,128)S(1)} copy-done((s32[16,32]{1,0:T(8,128)S(1)}, s32[16,32]{1,0:T(8,128)}, u32[]{:S(2)}) %copy-start.2) | copy-done | bytes 2072
  3.2 0.0 copy-start.3
  3.2 0.7 %copy-done.3 = s32[1,1152]{1,0:T(1,128)S(1)} copy-done((s32[1,1152]{1,0:T(1,128)S(1)}, s32[1,1152]{1,0:T(1,128)}, u32[]{:S(2)}) %copy-start.3) | copy-done | bytes 4632
  3.9 0.0 copy-start.4
  3.9 0.7 %copy-done.4 = s32[1,1152]{1,0:T(1,128)S(1)} copy-done((s32[1,1152]{1,0:T(1,128)S(1)}, s32[1,1152]{1,0:T(1,128)}, u32[]{:S(2)}) %copy-start.4) | copy-done | bytes 4632
  4.5 0.0 copy-start.5
  4.5 0.7 %copy-done.5 = s32[1,1152]{1,0:T(1,128)S(1)} copy-done((s32[1,1152]{1,0:T(1,128)S(1)}, s32[1,1152]{1,0:T(1,128)}, u32[]{:S(2)}) %copy-start.5) | copy-done | bytes 4632
  5.2 0.0 copy-start.6
  5.2 0.7 %copy-done.6 = f32[2,128]{1,0:T(2,128)S(1)} copy-done((f32[2,128]{1,0:T(2,128)S(1)}, f32[2,128]{1,0:T(2,128)}, u32[]{:S(2)}) %copy-start.6) | copy-done | bytes 1048
  5.9 28.3 %shard_map.73 = f32[512,64]{1,0:T(8,128)S(1)} custom-call(s32[1,1152]{1,0:T(1,128)S(1)} %copy-done.3, s32[1,1152]{1,0:T(1,128)S(1)} %copy-done.4, s32[1,1152]{1,0:T(1,128)S(1)} %copy-done.5, f32[2,128]{1,0:T(2,128)S(1)} %copy-done.6, s32[32,128]{1,0:T(8,128)S(1)} %copy-done.1, s32[16,32]{1,0:T(8,128)S(1)} %copy-done.2, bf16[1152,1152]{1,0:T(8,128)(2,1)S(1)} %bitcast.4), custom_call_target="tpu_custom_call" | custom-call | tf_op jit(solution)/shard_map/pallas_call | solution.py:488
  34.2 0.1 copy.9
  34.3 0.2 reshape.3
  34.5 1.0 %copy.10 = f32[2,16,32,32]{3,2,1,0:T(8,128)} copy(f32[2,16,32,32]{2,1,3,0:T(8,128)S(1)} %bitcast.5) | data formatting | bytes 262144 | tf_op jit(solution)/shard_map/transpose | solution.py:529
Async XLA Ops:
  0.0 1.7 %copy-start = (bf16[1,1152,1152]{2,1,0:T(8,128)(2,1)S(1)}, bf16[1,1152,1152]{2,1,0:T(8,128)(2,1)}, u32[]{:S(2)}) copy-start(bf16[1,1152,1152]{2,1,0:T(8,128)(2,1)} %param.7) | copy-start | bytes 7962628
  1.8 0.7 %copy-start.1 = (s32[32,128]{1,0:T(8,128)S(1)}, s32[32,128]{1,0:T(8,128)}, u32[]{:S(2)}) copy-start(s32[32,128]{1,0:T(8,128)} %plus_ref.1) | copy-start | bytes 49156
  2.5 0.7 %copy-start.2 = (s32[16,32]{1,0:T(8,128)S(1)}, s32[16,32]{1,0:T(8,128)}, u32[]{:S(2)}) copy-start(s32[16,32]{1,0:T(8,128)} %cross_ref.1) | copy-start | bytes 6148
  3.2 0.7 %copy-start.3 = (s32[1,1152]{1,0:T(1,128)S(1)}, s32[1,1152]{1,0:T(1,128)}, u32[]{:S(2)}) copy-start(s32[1,1152]{1,0:T(1,128)} %site_ref.1) | copy-start | bytes 13828
  3.9 0.7 %copy-start.4 = (s32[1,1152]{1,0:T(1,128)S(1)}, s32[1,1152]{1,0:T(1,128)}, u32[]{:S(2)}) copy-start(s32[1,1152]{1,0:T(1,128)} %time_ref.1) | copy-start | bytes 13828
  4.5 0.7 %copy-start.5 = (s32[1,1152]{1,0:T(1,128)S(1)}, s32[1,1152]{1,0:T(1,128)}, u32[]{:S(2)}) copy-start(s32[1,1152]{1,0:T(1,128)} %spin_ref.1) | copy-start | bytes 13828
  5.2 0.7 %copy-start.6 = (f32[2,128]{1,0:T(2,128)S(1)}, f32[2,128]{1,0:T(2,128)}, u32[]{:S(2)}) copy-start(f32[2,128]{1,0:T(2,128)} %free_ref.1) | copy-start | bytes 3076

commit v2 on v1

--- a/solution.py
+++ b/solution.py
@@ -156,14 +156,21 @@
 def kernel(
     nblk,
     ngroup,
+    site_hbm,
+    time_hbm,
+    spin_hbm,
+    free_hbm,
+    plus_hbm,
+    cross_hbm,
+    matrix_hbm,
+    out_ref,
     site_ref,
     time_ref,
     spin_ref,
     free_ref,
     plus_ref,
     cross_ref,
-    matrix_hbm,
-    out_ref,
+    total,
     matrix,
     rows,
     kern,
@@ -179,6 +186,7 @@
     halfway,
     tsend,
     trecv,
+    small_sem,
     matrix_sem,
     st_send,
     st_recv,
@@ -187,6 +195,22 @@
     t_send,
     t_recv,
 ):
+    small = [
+        pltpu.make_async_copy(source, target, small_sem.at[place])
+        for place, (source, target) in enumerate(
+            [
+                (site_hbm, site_ref),
+                (time_hbm, time_ref),
+                (spin_hbm, spin_ref),
+                (free_hbm, free_ref),
+                (plus_hbm, plus_ref),
+                (cross_hbm, cross_ref),
+            ]
+        )
+    ]
+    for copy in small:
+        copy.start()
+
     nz = nblk // INNER
     na = W // nblk
     nb = W // ngroup
@@ -223,6 +247,8 @@
     for index in range(CHUNKS):
         matrix_copy(index).start()
 
+    for copy in small:
+        copy.wait()
     site = site_ref[...]
     rx = site % LX
     ry = site // LX
@@ -456,11 +482,13 @@
     chunks = nq // nchunk
     lax.fori_loop(0, chunks, measure_chunk, 0)
 
-    out_ref[...] = dot_nt(sel_out[...], tsend[zz])
+    total[...] = dot_nt(sel_out[...], tsend[zz])
     for dz in range(1, nz):
         for chunk in range(chunks):
             t_copy(dz, chunk).wait_recv()
-        out_ref[...] += dot_nt(sel_out[...], trecv[dz])
+        total[...] += dot_nt(sel_out[...], trecv[dz])
+    for c in range(2):
+        out_ref[c] = total[:, c * nb : (c + 1) * nb].reshape(na, nq, nb)
 
     for slot, (dy, dg) in enumerate(plane):
         st_copy(slot + 1, dy, dg).wait_send()
@@ -485,12 +513,19 @@
     chunks = nq // (W // na)
     vmem = pl.BlockSpec(memory_space=pltpu.VMEM)
     dma = pltpu.SemaphoreType.DMA
-    out = pl.pallas_call(
+    return pl.pallas_call(
         functools.partial(kernel, nblk, ngroup),
-        out_shape=jax.ShapeDtypeStruct((na * nq, 2 * nb), F32),
-        in_specs=[vmem] * 6 + [pl.BlockSpec(memory_space=pl.ANY)],
+        out_shape=jax.ShapeDtypeStruct((2, na, nq, nb), F32),
+        in_specs=[pl.BlockSpec(memory_space=pltpu.HBM)] * 7,
         out_specs=vmem,
         scratch_shapes=[
+            pltpu.VMEM(vertex_site.shape, jnp.int32),
+            pltpu.VMEM(vertex_time.shape, jnp.int32),
+            pltpu.VMEM(vertex_spin.shape, jnp.int32),
+            pltpu.VMEM(free_green.shape, F32),
+            pltpu.VMEM(plus_table.shape, jnp.int32),
+            pltpu.VMEM(cross_table.shape, jnp.int32),
+            pltpu.VMEM((na * nq, 2 * nb), F32),
             pltpu.VMEM((nv, nv), BF),
             pltpu.VMEM((4 * W, nv), BF),
             pltpu.VMEM((2, 2 * W, 2 * W), F32),
@@ -506,6 +541,7 @@
             pltpu.VMEM((npair, nw, 2, nb, 2 * W), BF),
             pltpu.VMEM((nz, 2 * nb, nq * na), BF),
             pltpu.VMEM((nz, 2 * nb, nq * na), BF),
+            dma((6,)),
             dma((CHUNKS,)),
             dma((nw,)),
             dma((nw,)),
@@ -515,7 +551,7 @@
             dma((nz, chunks)),
         ],
         compiler_params=pltpu.CompilerParams(
-            collective_id=0, has_side_effects=True, vmem_limit_bytes=40 * 1024 * 1024
+            collective_id=0, has_side_effects=True, vmem_limit_bytes=63 * 1024 * 1024
         ),
     )(
         vertex_site,
@@ -526,7 +562,6 @@
         cross_table,
         vertex_matrix[0],
     )
-    return out.reshape(na, nq, 2, nb).transpose(2, 0, 1, 3)
 
 
 def fits(mesh):

time: 36 us -> 31.8 us (0.88)
  local copies, waits for them, and re-layouts: 7.23 us -> 1.87 us
  Pallas kernels: 28.3 us -> 29.8 us
    unnamed x14 -> x1, local copies, waits for them, and re-layouts: 5.9 us -> 1.87 us
    pallas_call x1, Pallas kernels: 28.3 us -> 29.8 us  [kernel_body(): pl.pallas_call(functools.partial(kernel, nblk, ngroup), out_shape=jax.Sha...]
    transpose x1 -> x0, local copies, waits for them, and re-layouts: 1.05 us -> none  [kernel_body(): return out.reshape(na, nq, 2, nb).transpose(2, 0, 1, 3)]
where the time goes in v2:
time: 31.8 us; the launch traced here: 31.6 us
  Pallas kernels  29.8 us (94%)
  local copies, waits for them, and re-layouts  1.87 us (6%)
    pallas_call x1, Pallas kernels, kernel_body(): pl.pallas_call(functools.partial(kernel, nblk, ngroup), out_shape=jax.Sha...  29.8 us
    unnamed x1, local copies, waits for them, and re-layouts  1.87 us

profile of v2, /device:TPU:0, one launch (start us, length us, event | category | flops | bytes accessed | tf_op | source)
XLA Modules:
  0.0 31.6 jit_solution(14335509396839457632)
XLA Ops:
  0.0 29.8 %shard_map.73 = f32[2,16,32,32]{3,2,1,0:T(8,128)} custom-call(s32[1,1152]{1,0:T(1,128)} %site_hbm.1, s32[1,1152]{1,0:T(1,128)} %time_hbm.1, s32[1,1152]{1,0:T(1,128)} %spin_hbm.1, f32[2,128]{1,0:T(2,128)} %free_hbm.1, s32[32,128]{1,0:T(8,128)} %plus_hbm.1, s32[16,32]{1,0:T(8,128)} %cross_hbm.1, bf16[1152,1152]{1,0:T(8,128)(2,1)} %bitcast.1), custom_call_target="tpu_custom_call" | custom-call | tf_op jit(solution)/shard_map/pallas_call | solution.py:516
  29.8 1.9 %copy.9 = f32[2,16,32,32]{3,2,1,0:T(8,128)} copy(f32[2,16,32,32]{3,2,1,0:T(8,128)} %shard_map.73) | data formatting | bytes 262144

commit v3 on v2

--- a/solution.py
+++ b/solution.py
@@ -133,12 +133,17 @@
 F32 = jnp.float32
 MESH = pl.DeviceIdType.MESH
 INNER = 2
+CORES = 2
 PARTS = 4
 CHUNKS = 3
 
 
 def iota(shape, dim):
     return lax.broadcasted_iota(jnp.int32, shape, dim)
+
+
+def shift_down(value, divisor):
+    return value >> (divisor.bit_length() - 1)
 
 
 def one_hot(condition):
@@ -224,17 +229,25 @@
     grp = lax.axis_index("group")
     zz = blk // INNER
     yy = blk % INNER
-    plane = [(dy, dg) for dy in range(INNER) for dg in range(ngroup) if dy + dg > 0]
-
-    def plane_peer(dy, dg):
-        return (zz * INNER + (yy + dy) % INNER, (grp + dg) % ngroup)
+    nx = ngroup // CORES
+    xx = grp // CORES
+    core = grp % CORES
+    near = nx * INNER
+    plane = list(range(1, CORES * near))
+
+    def plane_peer(slot):
+        dc, dy, dx = slot // near, slot // nx % INNER, slot % nx
+        return (
+            zz * INNER + (yy + dy) % INNER,
+            (xx + dx) % nx * CORES + (core + dc) % CORES,
+        )
 
     def z_peer(dz):
         return (((zz + dz) % nz) * INNER + yy, grp)
 
     barrier = pltpu.get_barrier_semaphore()
-    for dy, dg in plane:
-        pl.semaphore_signal(barrier, inc=1, device_id=plane_peer(dy, dg), device_id_type=MESH)
+    for slot in plane:
+        pl.semaphore_signal(barrier, inc=1, device_id=plane_peer(slot), device_id_type=MESH)
     for dz in range(1, nz):
         pl.semaphore_signal(barrier, inc=1, device_id=z_peer(dz), device_id_type=MESH)
 
@@ -249,38 +262,51 @@
 
     for copy in small:
         copy.wait()
-    site = site_ref[...]
-    rx = site % LX
-    ry = site // LX
-    freq = iota((NW, nv), 0)
-    winding = ((2 * freq + 1) * time_ref[...]) % (2 * NT)
-    angles = winding.astype(F32) * (math.pi / NT)
-    cosine = jnp.cos(angles)
-    sine = jnp.sin(angles)
-    spin = jnp.broadcast_to(spin_ref[...], (NW, nv))
-    up = jnp.where(spin == 0, 1.0, 0.0)
-    down = jnp.where(spin == 1, 1.0, 0.0)
-    rx = jnp.broadcast_to(rx, (NW, nv))
-    ry = jnp.broadcast_to(ry, (NW, nv))
-    for first in range(0, W // NW, 2):
-        c_rows = []
-        s_rows = []
-        for k in (first, first + 1):
-            turn = ((k % LX) * rx + (k // LX) * ry) % 4
-            odd = turn % 2 == 1
-            c_sign = jnp.where((turn == 1) | (turn == 2), -1.0, 1.0)
-            s_sign = jnp.where(turn >= 2, -1.0, 1.0)
-            c_rows.append(jnp.where(odd, sine, cosine) * c_sign)
-            s_rows.append(jnp.where(odd, cosine, sine) * s_sign)
-        both_up = jnp.concatenate([up, up], 0)
-        both_down = jnp.concatenate([down, down], 0)
-        c_both = jnp.concatenate(c_rows, 0)
-        s_both = jnp.concatenate(s_rows, 0)
-        at = first * NW
-        rows[pl.ds(at, 2 * NW), :] = (c_both * both_up).astype(BF)
-        rows[pl.ds(W + at, 2 * NW), :] = (s_both * both_up).astype(BF)
-        rows[pl.ds(2 * W + at, 2 * NW), :] = (c_both * both_down).astype(BF)
-        rows[pl.ds(3 * W + at, 2 * NW), :] = (s_both * both_down).astype(BF)
+
+    quarter = NT // 2
+    site = jnp.broadcast_to(site_ref[...], (2 * NW, nv))
+    rx = site & (LX - 1)
+    ry = shift_down(site, LX)
+    ids = iota((2 * NW, nv), 0)
+    freq = ids & (NW - 1)
+    upper = shift_down(ids, NW)
+    winding = (2 * freq + 1) * time_ref[...]
+    turns = shift_down(winding + quarter // 2, quarter)
+    rest = (winding - turns * quarter).astype(F32) * (math.pi / NT)
+    square = rest * rest
+    cosine = 1.0 + square * (
+        -1 / 2
+        + square
+        * (1 / 24 + square * (-1 / 720 + square * (1 / 40320 + square * (-1 / 3628800))))
+    )
+    sine = rest + rest * square * (
+        -1 / 6 + square * (1 / 120 + square * (-1 / 5040 + square * (1 / 362880)))
+    )
+    cosine = cosine.astype(BF)
+    sine = sine.astype(BF)
+
+    def unit(amount):
+        amount = amount & 3
+        real = jnp.where(amount == 0, 1.0, jnp.where(amount == 2, -1.0, 0.0))
+        imag = jnp.where(amount == 1, 1.0, jnp.where(amount == 3, -1.0, 0.0))
+        return real.astype(BF), imag.astype(BF)
+
+    def turn(value, by):
+        return (value[0] * by[0] - value[1] * by[1], value[1] * by[0] + value[0] * by[1])
+
+    spin = jnp.broadcast_to(spin_ref[...], (2 * NW, nv))
+    up = one_hot(spin == 0)
+    down = one_hot(spin == 1)
+    across = [unit((kx + upper) * rx) for kx in range(0, LX, 2)]
+    for ky in range(W // NW // LX):
+        base = turn((cosine, sine), unit(turns + ky * ry))
+        for place, by in enumerate(across):
+            c_both, s_both = turn(base, by)
+            at = (ky * LX + 2 * place) * NW
+            rows[pl.ds(at, 2 * NW), :] = c_both * up
+            rows[pl.ds(W + at, 2 * NW), :] = s_both * up
+            rows[pl.ds(2 * W + at, 2 * NW), :] = c_both * down
+            rows[pl.ds(3 * W + at, 2 * NW), :] = s_both * down
 
     kern[...] = jnp.zeros_like(kern)
 
@@ -316,38 +342,40 @@
 
     pl.semaphore_wait(barrier, len(plane) + nz - 1)
 
-    def st_copy(slot, dy, dg):
+    def st_copy(source, slot, steps):
         return pltpu.make_async_remote_copy(
-            src_ref=st.at[0],
+            src_ref=st.at[source],
             dst_ref=st.at[slot],
             send_sem=st_send.at[slot],
             recv_sem=st_recv.at[slot],
-            device_id=plane_peer(dy, dg),
+            device_id=plane_peer(steps),
             device_id_type=MESH,
         )
 
-    def lr_copy(slot, dy, dg):
-        wanted = ((yy + dy) % INNER) * ngroup + (grp + dg) % ngroup
+    def lr_copy(slot):
+        peer = plane_peer(slot)
+        wanted = peer[0] % INNER * ngroup + peer[1]
         return pltpu.make_async_remote_copy(
             src_ref=lr_send.at[wanted],
             dst_ref=lr.at[slot],
             send_sem=lr_send_sem.at[slot],
             recv_sem=lr_recv.at[slot],
-            device_id=plane_peer(dy, dg),
+            device_id=peer,
             device_id_type=MESH,
         )
 
-    for slot, (dy, dg) in enumerate(plane):
-        st_copy(slot + 1, dy, dg).start()
+    for slot in range(near - 1, 0, -1):
+        st_copy(0, slot, slot).start()
+    st_copy(0, near, near).start()
 
     greens = [g.astype(BF).astype(F32) for g in greens]
     turned = [g.astype(BF).astype(F32) for g in turned]
     plus = plus_ref[...].astype(F32)
     plus_turned = jnp.concatenate([plus, jnp.zeros((W - nq, W), F32)], 0).T
-    expand = one_hot(iota((W, W), 1) // PARTS == iota((W, W), 0))
+    expand = one_hot(shift_down(iota((W, W), 1), PARTS) == iota((W, W), 0))
     index = dot(plus_turned.astype(BF), expand).astype(jnp.int32)
     lane = iota((W, W), 1)
-    part = lane % PARTS
+    part = lane & (PARTS - 1)
 
     def choose(values):
         picked = values[0]
@@ -373,8 +401,8 @@
         for y in range(INNER):
             joined = jnp.where(lane < half, left, shifted(lead, half - half * y))
             lr_send[y * ngroup + j] = joined.astype(BF)
-    for slot, (dy, dg) in enumerate(plane):
-        lr_copy(slot + 1, dy, dg).start()
+    for slot in plane:
+        lr_copy(slot).start()
     lr[0] = lr_send[yy * ngroup + grp]
 
     plus_bf = plus.astype(BF)
@@ -383,7 +411,7 @@
     for q in range(nq):
         column = jnp.broadcast_to(plus_b[:, q : q + 1], (nb, W))
         sel_b[pl.ds(q * nb, nb), :] = one_hot(column == iota((nb, W), 1))
-    place = (lane % half) // na * (na * INNER) + na * yy + lane % na
+    place = shift_down(lane & (half - 1), na) * (na * INNER) + na * yy + (lane & (na - 1))
     my_a = one_hot(iota((W, W), 0) == place)
     prow[...] = dot(plus_bf, my_a)
 
@@ -402,7 +430,11 @@
 
     width = nz * W
     source = iota((width, W), 0)
-    target = (source // na) % nz * W + source // half * na + source % na
+    target = (
+        (shift_down(source, na) & (nz - 1)) * W
+        + shift_down(source, half) * na
+        + (source & (na - 1))
+    )
     for z in range(nz):
         spread[:, z * W : (z + 1) * W] = one_hot(target == iota((width, W), 1) + z * W)
 
@@ -412,11 +444,7 @@
         column = jnp.broadcast_to(crossing[:, r : r + 1] * na + r, (nq, nq * na))
         sel_out[pl.ds(r * nq, nq), :] = one_hot(column == iota((nq, nq * na), 1))
 
-    def first_selection(slot, carry):
-        @pl.when(slot > 0)
-        def _():
-            st_copy(slot, 0, 1).wait_recv()
-
+    def first_selection(slot):
         for c in range(2):
             mine = st[slot, pl.ds(pl.multiple_of(c * W + nb * grp, nb), nb), :]
             sb[slot, c] = dot(mine, my_a)
@@ -425,12 +453,32 @@
                 halfway[q // 2, slot, c, :, pl.ds((q % 2) * W, W)] = chosen[
                     q * nb : (q + 1) * nb
                 ]
+
+    def own_chip(step, carry):
+        @pl.when(step > 0)
+        def _():
+            st_copy(0, near, near).wait_recv()
+
+        first_selection(step * near)
         return carry
 
-    lax.fori_loop(0, len(plane) + 1, first_selection, 0)
-
-    for slot, (dy, dg) in enumerate(plane):
-        lr_copy(slot + 1, dy, dg).wait_recv()
+    def same_core(step, carry):
+        st_copy(0, step, near).wait_recv()
+        st_copy(step, near + step, near).start()
+        first_selection(step)
+        return carry
+
+    def forwarded(step, carry):
+        st_copy(0, step, near).wait_recv()
+        first_selection(step)
+        return carry
+
+    lax.fori_loop(0, CORES, own_chip, 0)
+    lax.fori_loop(1, near, same_core, 0)
+    lax.fori_loop(near + 1, CORES * near, forwarded, 0)
+
+    for slot in plane:
+        lr_copy(slot).wait_recv()
 
     nw = len(plane) + 1
     four = W // (nw * PARTS)
@@ -446,6 +494,8 @@
             device_id=z_peer(dz),
             device_id_type=MESH,
         )
+
+    same_q = shift_down(iota((W, W), 0) & (depth - 1), PARTS) - shift_down(lane, half)
 
     def measure_chunk(chunk, carry):
         totals = []
@@ -467,8 +517,7 @@
                 stacked = lr[:, pl.ds(start, depth), :].reshape(W, W).astype(F32)
                 trailing = stacked.T[:half].astype(BF)
                 leading = jnp.where(lane < half, pltpu.roll(stacked, half, 1), stacked)
-                row_q = iota((W, W), 0) % depth // PARTS
-            masked = jnp.where(row_q == 2 * (sub % pairs) + lane // half, leading, 0.0)
+            masked = jnp.where(same_q == 2 * (sub % pairs), leading, 0.0)
             exchange = dot(trailing, masked.astype(BF))
             totals.append((jnp.concatenate([t_re, t_im], 0) - exchange).astype(BF))
         moved = dot(jnp.concatenate(totals, 1), spread[...]).astype(BF)
@@ -490,9 +539,9 @@
     for c in range(2):
         out_ref[c] = total[:, c * nb : (c + 1) * nb].reshape(na, nq, nb)
 
-    for slot, (dy, dg) in enumerate(plane):
-        st_copy(slot + 1, dy, dg).wait_send()
-        lr_copy(slot + 1, dy, dg).wait_send()
+    for slot in plane:
+        st_copy(0, slot, near).wait_send()
+        lr_copy(slot).wait_send()
     for dz in range(1, nz):
         for chunk in range(chunks):
             t_copy(dz, chunk).wait_send()
@@ -569,7 +618,7 @@
     if nblk % INNER or W % nblk or W % ngroup:
         return False
     nz, na, nb = nblk // INNER, W // nblk, W // ngroup
-    return nz == 4 and 2 * nz * na == W and 4 * nb == W and na % 16 == 0 and nb % 16 == 0
+    return nz == 4 and ngroup % CORES == 0 and 2 * nz * na == W and 4 * nb == W and na % 16 == 0 and nb % 16 == 0
 
 
 def solution(mesh):

time: 31.8 us -> 28.4 us (0.89)
  Pallas kernels: 29.8 us -> 26.3 us
    pallas_call x1, Pallas kernels: 29.8 us -> 26.3 us  [kernel_body(): pl.pallas_call(functools.partial(kernel, nblk, ngroup), out_shape=jax.Sha...]
where the time goes in v3:
time: 28.4 us; the launch traced here: 28.2 us
  Pallas kernels  26.3 us (93%)
  local copies, waits for them, and re-layouts  1.87 us (7%)
    pallas_call x1, Pallas kernels, kernel_body(): pl.pallas_call(functools.partial(kernel, nblk, ngroup), out_shape=jax.Sha...  26.3 us
    unnamed x1, local copies, waits for them, and re-layouts  1.87 us

profile of v3, /device:TPU:0, one launch (start us, length us, event | category | flops | bytes accessed | tf_op | source)
XLA Modules:
  0.0 28.2 jit_solution(16418927925218618331)
XLA Ops:
  0.0 26.3 %shard_map.73 = f32[2,16,32,32]{3,2,1,0:T(8,128)} custom-call(s32[1,1152]{1,0:T(1,128)} %site_hbm.1, s32[1,1152]{1,0:T(1,128)} %time_hbm.1, s32[1,1152]{1,0:T(1,128)} %spin_hbm.1, f32[2,128]{1,0:T(2,128)} %free_hbm.1, s32[32,128]{1,0:T(8,128)} %plus_hbm.1, s32[16,32]{1,0:T(8,128)} %cross_hbm.1, bf16[1152,1152]{1,0:T(8,128)(2,1)} %bitcast.1), custom_call_target="tpu_custom_call" | custom-call | tf_op jit(solution)/shard_map/pallas_call | solution.py:565
  26.3 1.9 %copy.9 = f32[2,16,32,32]{3,2,1,0:T(8,128)} copy(f32[2,16,32,32]{3,2,1,0:T(8,128)} %shard_map.73) | data formatting | bytes 262144

commit v4 on v3

--- a/solution.py
+++ b/solution.py
@@ -134,6 +134,7 @@
 MESH = pl.DeviceIdType.MESH
 INNER = 2
 CORES = 2
+VMEM_BYTES = 64 * 1024 * 1024
 PARTS = 4
 CHUNKS = 3
 
@@ -175,7 +176,6 @@
     free_ref,
     plus_ref,
     cross_ref,
-    total,
     matrix,
     rows,
     kern,
@@ -185,7 +185,6 @@
     sel_b,
     sel_a,
     sel_out,
-    spread,
     prow,
     sb,
     halfway,
@@ -352,17 +351,19 @@
             device_id_type=MESH,
         )
 
-    def lr_copy(slot):
-        peer = plane_peer(slot)
-        wanted = peer[0] % INNER * ngroup + peer[1]
+    def lr_copy(source, slot, steps):
         return pltpu.make_async_remote_copy(
-            src_ref=lr_send.at[wanted],
+            src_ref=source,
             dst_ref=lr.at[slot],
             send_sem=lr_send_sem.at[slot],
             recv_sem=lr_recv.at[slot],
-            device_id=peer,
+            device_id=plane_peer(steps),
             device_id_type=MESH,
         )
+
+    def lr_for(slot):
+        dy, dx = slot // nx % INNER, slot % nx
+        return lr_send.at[(yy + dy) % INNER * nx + (xx + dx) % nx]
 
     for slot in range(near - 1, 0, -1):
         st_copy(0, slot, slot).start()
@@ -385,8 +386,7 @@
 
     lead = choose([jnp.take_along_axis(g, index, axis=1) for g in greens])
     trail = [jnp.take_along_axis(g, index, axis=1) for g in turned]
-    trail_re = choose([trail[0], -trail[1], trail[2], -trail[3]]).T
-    trail_im = choose([trail[1], trail[0], trail[3], trail[2]]).T
+    trail = choose(trail).T
     order = [INNER * z + y for y in range(INNER) for z in range(nz)]
     lead = jnp.concatenate([lead[na * i : na * (i + 1)] for i in order], 0).T
 
@@ -394,16 +394,15 @@
         by = by % W
         return value if by == 0 else pltpu.roll(value, by, 1)
 
-    for j in range(ngroup):
-        left = jnp.where(
-            lane < nb, shifted(trail_re, -nb * j), shifted(trail_im, nb - nb * j)
-        )
+    for x in range(nx):
+        left = shifted(trail, -half * x)
         for y in range(INNER):
             joined = jnp.where(lane < half, left, shifted(lead, half - half * y))
-            lr_send[y * ngroup + j] = joined.astype(BF)
-    for slot in plane:
-        lr_copy(slot).start()
-    lr[0] = lr_send[yy * ngroup + grp]
+            lr_send[y * nx + x] = joined.astype(BF)
+    for slot in range(near - 1, 0, -1):
+        lr_copy(lr_for(slot), slot, slot).start()
+    lr_copy(lr_for(near), near, near).start()
+    lr[0] = lr_send[yy * nx + xx]
 
     plus_bf = plus.astype(BF)
     my_b = one_hot(iota((nb, W), 1) == iota((nb, W), 0) + nb * grp)
@@ -428,20 +427,15 @@
 
     lax.fori_loop(0, npair, pair_selector, 0)
 
-    width = nz * W
-    source = iota((width, W), 0)
-    target = (
-        (shift_down(source, na) & (nz - 1)) * W
-        + shift_down(source, half) * na
-        + (source & (na - 1))
-    )
-    for z in range(nz):
-        spread[:, z * W : (z + 1) * W] = one_hot(target == iota((width, W), 1) + z * W)
-
     same = one_hot(iota((nq, nq), 0) == iota((nq, nq), 1))
     crossing = dot_nt(same, cross_ref[...].astype(F32).astype(BF)).astype(jnp.int32)
+    crossing = (
+        shift_down(crossing, nchunk) * W
+        + (crossing & 1) * half
+        + (shift_down(crossing, 2) & (nz - 1)) * na
+    )
     for r in range(na):
-        column = jnp.broadcast_to(crossing[:, r : r + 1] * na + r, (nq, nq * na))
+        column = jnp.broadcast_to(crossing[:, r : r + 1] + r, (nq, nq * na))
         sel_out[pl.ds(r * nq, nq), :] = one_hot(column == iota((nq, nq * na), 1))
 
     def first_selection(slot):
@@ -475,10 +469,13 @@
 
     lax.fori_loop(0, CORES, own_chip, 0)
     lax.fori_loop(1, near, same_core, 0)
+    for slot in range(1, near):
+        lr_copy(lr.at[0], slot, near).wait_recv()
+        lr_copy(lr.at[slot], near + slot, near).start()
     lax.fori_loop(near + 1, CORES * near, forwarded, 0)
 
-    for slot in plane:
-        lr_copy(slot).wait_recv()
+    for slot in range(near, CORES * near):
+        lr_copy(lr.at[0], slot, near).wait_recv()
 
     nw = len(plane) + 1
     four = W // (nw * PARTS)
@@ -515,15 +512,27 @@
             if sub % pairs == 0:
                 start = pl.multiple_of((chunk * (nz // pairs) + sub // pairs) * depth, depth)
                 stacked = lr[:, pl.ds(start, depth), :].reshape(W, W).astype(F32)
-                trailing = stacked.T[:half].astype(BF)
+                turned_back = stacked.T
+                mine = jnp.where(core == 0, turned_back[:nb], turned_back[nb : 2 * nb])
+                odd = (iota((nb, W), 1) & 1) == 1
+                trailing = jnp.concatenate(
+                    [
+                        jnp.where(odd, -mine, mine),
+                        jnp.where(odd, pltpu.roll(mine, 1, 1), pltpu.roll(mine, W - 1, 1)),
+                    ],
+                    0,
+                ).astype(BF)
                 leading = jnp.where(lane < half, pltpu.roll(stacked, half, 1), stacked)
             masked = jnp.where(same_q == 2 * (sub % pairs), leading, 0.0)
             exchange = dot(trailing, masked.astype(BF))
-            totals.append((jnp.concatenate([t_re, t_im], 0) - exchange).astype(BF))
-        moved = dot(jnp.concatenate(totals, 1), spread[...]).astype(BF)
+            totals.append(jnp.concatenate([t_re, t_im], 0) - exchange)
+        spot = shift_down(iota((2 * nb, W), 1), na) & (nz - 1)
         cols = pl.ds(pl.multiple_of(chunk * W, W), W)
         for z in range(nz):
-            tsend[z, :, cols] = moved[:, z * W : (z + 1) * W]
+            moved = shifted(totals[0], -na * z)
+            for sub in range(1, nz):
+                moved = jnp.where(spot == sub, shifted(totals[sub], na * (sub - z)), moved)
+            tsend[z, :, cols] = moved.astype(BF)
         for dz in range(1, nz):
             t_copy(dz, chunk).start()
         return carry
@@ -531,17 +540,16 @@
     chunks = nq // nchunk
     lax.fori_loop(0, chunks, measure_chunk, 0)
 
-    total[...] = dot_nt(sel_out[...], tsend[zz])
+    total = dot_nt(tsend[zz], sel_out[...])
     for dz in range(1, nz):
         for chunk in range(chunks):
             t_copy(dz, chunk).wait_recv()
-        total[...] += dot_nt(sel_out[...], trecv[dz])
-    for c in range(2):
-        out_ref[c] = total[:, c * nb : (c + 1) * nb].reshape(na, nq, nb)
+        total = total + dot_nt(trecv[dz], sel_out[...])
+    out_ref[...] = total
 
     for slot in plane:
         st_copy(0, slot, near).wait_send()
-        lr_copy(slot).wait_send()
+        lr_copy(lr.at[0], slot, near).wait_send()
     for dz in range(1, nz):
         for chunk in range(chunks):
             t_copy(dz, chunk).wait_send()
@@ -562,9 +570,9 @@
     chunks = nq // (W // na)
     vmem = pl.BlockSpec(memory_space=pltpu.VMEM)
     dma = pltpu.SemaphoreType.DMA
-    return pl.pallas_call(
+    out = pl.pallas_call(
         functools.partial(kernel, nblk, ngroup),
-        out_shape=jax.ShapeDtypeStruct((2, na, nq, nb), F32),
+        out_shape=jax.ShapeDtypeStruct((2 * nb, na * nq), F32),
         in_specs=[pl.BlockSpec(memory_space=pltpu.HBM)] * 7,
         out_specs=vmem,
         scratch_shapes=[
@@ -574,17 +582,15 @@
             pltpu.VMEM(free_green.shape, F32),
             pltpu.VMEM(plus_table.shape, jnp.int32),
             pltpu.VMEM(cross_table.shape, jnp.int32),
-            pltpu.VMEM((na * nq, 2 * nb), F32),
             pltpu.VMEM((nv, nv), BF),
             pltpu.VMEM((4 * W, nv), BF),
             pltpu.VMEM((2, 2 * W, 2 * W), F32),
             pltpu.VMEM((nw, 2 * W, W), BF),
             pltpu.VMEM((nw, W, W), BF),
-            pltpu.VMEM((nw, W, W), BF),
+            pltpu.VMEM((nw // CORES, W, W), BF),
             pltpu.VMEM((nq * nb, W), BF),
             pltpu.VMEM((npair, 2 * W, W), BF),
             pltpu.VMEM((na * nq, nq * na), BF),
-            pltpu.VMEM((nz * W, nz * W), BF),
             pltpu.VMEM((nq, W), F32),
             pltpu.VMEM((nw, 2, nb, W), F32),
             pltpu.VMEM((npair, nw, 2, nb, 2 * W), BF),
@@ -600,7 +606,7 @@
             dma((nz, chunks)),
         ],
         compiler_params=pltpu.CompilerParams(
-            collective_id=0, has_side_effects=True, vmem_limit_bytes=63 * 1024 * 1024
+            collective_id=0, has_side_effects=True, vmem_limit_bytes=VMEM_BYTES - 1024 * 1024
         ),
     )(
         vertex_site,
@@ -611,6 +617,7 @@
         cross_table,
         vertex_matrix[0],
     )
+    return out.reshape(2, nb, na, nq).transpose(0, 2, 3, 1)
 
 
 def fits(mesh):

time: 28.4 us -> 28 us (0.986)
  Pallas kernels: 26.3 us -> 25.7 us
    reshape x0 -> x2, local copies, waits for them, and re-layouts: none -> 2.12 us  [kernel_body(): return out.reshape(2, nb, na, nq).transpose(0, 2, 3, 1)]
    unnamed x1 -> x0, local copies, waits for them, and re-layouts: 1.87 us -> none
    pallas_call x1, Pallas kernels: 26.3 us -> 25.7 us  [kernel_body(): pl.pallas_call(functools.partial(kernel, nblk, ngroup), out_shape=jax.Sha...]
where the time goes in v4:
time: 28 us; the launch traced here: 27.8 us
  Pallas kernels  25.7 us (92%)
  local copies, waits for them, and re-layouts  2.12 us (8%)
    pallas_call x1, Pallas kernels, kernel_body(): pl.pallas_call(functools.partial(kernel, nblk, ngroup), out_shape=jax.Sha...  25.7 us
    reshape x2, local copies, waits for them, and re-layouts, kernel_body(): return out.reshape(2, nb, na, nq).transpose(0, 2, 3, 1)  2.12 us

profile of v4, /device:TPU:0, one launch (start us, length us, event | category | flops | bytes accessed | tf_op | source)
XLA Modules:
  0.0 27.8 jit_solution(2665438052502723428)
XLA Ops:
  0.0 25.7 %shard_map.73 = f32[64,512]{1,0:T(8,128)} custom-call(s32[1,1152]{1,0:T(1,128)} %site_hbm.1, s32[1,1152]{1,0:T(1,128)} %time_hbm.1, s32[1,1152]{1,0:T(1,128)} %spin_hbm.1, f32[2,128]{1,0:T(2,128)} %free_hbm.1, s32[32,128]{1,0:T(8,128)} %plus_hbm.1, s32[16,32]{1,0:T(8,128)} %cross_hbm.1, bf16[1152,1152]{1,0:T(8,128)(2,1)} %bitcast.2), custom_call_target="tpu_custom_call" | custom-call | tf_op jit(solution)/shard_map/pallas_call | solution.py:573
  25.7 1.1 %reshape.3 = f32[2,32,16,32]{3,2,1,0:T(8,128)S(1)} reshape(f32[64,512]{1,0:T(8,128)} %shard_map.73) | data formatting | bytes 262144 | tf_op jit(solution)/shard_map/reshape | solution.py:620
  26.8 1.0 %copy.8 = f32[2,32,16,32]{1,3,2,0:T(8,128)} copy(f32[2,32,16,32]{3,2,1,0:T(8,128)S(1)} %reshape.3) | data formatting | bytes 262144 | tf_op jit(solution)/shard_map/reshape | solution.py:620

commit v5 on v4

--- a/solution.py
+++ b/solution.py
@@ -136,7 +136,7 @@
 CORES = 2
 VMEM_BYTES = 64 * 1024 * 1024
 PARTS = 4
-CHUNKS = 3
+PIECE = 256
 
 
 def iota(shape, dim):
@@ -223,7 +223,8 @@
     npair = nq // 2
     nchunk = W // na
     nv = site_ref.shape[1]
-    piece = nv // CHUNKS
+    pieces = nv // PIECE
+    tail = nv % PIECE
     blk = lax.axis_index("blk")
     grp = lax.axis_index("group")
     zz = blk // INNER
@@ -244,20 +245,23 @@
     def z_peer(dz):
         return (((zz + dz) % nz) * INNER + yy, grp)
 
+    def matrix_copy(index, width):
+        cols = pl.ds(index * PIECE, width)
+        return pltpu.make_async_copy(
+            matrix_hbm.at[:, cols], matrix.at[:, cols], matrix_sem.at[index]
+        )
+
+
+    for index in range(pieces):
+        matrix_copy(index, PIECE).start()
+    if tail:
+        matrix_copy(pieces, tail).start()
+
     barrier = pltpu.get_barrier_semaphore()
     for slot in plane:
         pl.semaphore_signal(barrier, inc=1, device_id=plane_peer(slot), device_id_type=MESH)
     for dz in range(1, nz):
         pl.semaphore_signal(barrier, inc=1, device_id=z_peer(dz), device_id_type=MESH)
-
-    def matrix_copy(index):
-        cols = pl.ds(pl.multiple_of(index * piece, 128), piece)
-        return pltpu.make_async_copy(
-            matrix_hbm.at[:, cols], matrix.at[:, cols], matrix_sem.at[index]
-        )
-
-    for index in range(CHUNKS):
-        matrix_copy(index).start()
 
     for copy in small:
         copy.wait()
@@ -309,17 +313,23 @@
 
     kern[...] = jnp.zeros_like(kern)
 
-    def project(index, carry):
-        matrix_copy(index).wait()
-        cols = pl.ds(pl.multiple_of(index * piece, 128), piece)
+    def project(index, width):
+        matrix_copy(index, width).wait()
+        start = index * PIECE
+        cols = pl.ds(start if isinstance(start, int) else pl.multiple_of(start, PIECE), width)
         projected = dot(rows[...], matrix[:, cols]).astype(BF)
         for s in range(2):
             kern[s] += dot_nt(
                 projected[2 * W * s : 2 * W * (s + 1)], rows[pl.ds(2 * W * s, 2 * W), cols]
             )
+
+    def project_piece(index, carry):
+        project(index, PIECE)
         return carry
 
-    lax.fori_loop(0, CHUNKS, project, 0)
+    lax.fori_loop(0, pieces, project_piece, 0)
+    if tail:
+        project(pieces, tail)
 
     ga_re = jnp.broadcast_to(free_ref[0:1, :], (W, W))
     ga_im = jnp.broadcast_to(free_ref[1:2, :], (W, W))
@@ -438,15 +448,24 @@
         column = jnp.broadcast_to(crossing[:, r : r + 1] + r, (nq, nq * na))
         sel_out[pl.ds(r * nq, nq), :] = one_hot(column == iota((nq, nq * na), 1))
 
-    def first_selection(slot):
+    def take_rows(slot):
         for c in range(2):
             mine = st[slot, pl.ds(pl.multiple_of(c * W + nb * grp, nb), nb), :]
             sb[slot, c] = dot(mine, my_a)
-            chosen = dot_nt(sel_b[...], st[slot, c * W : (c + 1) * W, :]).astype(BF)
-            for q in range(nq):
-                halfway[q // 2, slot, c, :, pl.ds((q % 2) * W, W)] = chosen[
-                    q * nb : (q + 1) * nb
+
+    def select(slot, pair, count):
+        picks = sel_b[pl.ds(pl.multiple_of(pair * 2 * nb, 2 * nb), count * nb), :]
+        picked = dot_nt(picks, st[slot]).astype(BF)
+        for q in range(count):
+            for c in range(2):
+                halfway[pair + q // 2, slot, c, :, pl.ds((q % 2) * W, W)] = picked[
+                    q * nb : (q + 1) * nb, c * W : (c + 1) * W
                 ]
+
+    def first_selection(slot):
+        take_rows(slot)
+        for chunk in range(nq // nchunk):
+            select(slot, chunk * nchunk // 2, nchunk)
 
     def own_chip(step, carry):
         @pl.when(step > 0)
@@ -464,7 +483,7 @@
 
     def forwarded(step, carry):
         st_copy(0, step, near).wait_recv()
-        first_selection(step)
+        take_rows(step)
         return carry
 
     lax.fori_loop(0, CORES, own_chip, 0)
@@ -496,6 +515,8 @@
 
     def measure_chunk(chunk, carry):
         totals = []
+        for slot in range(near + 1, CORES * near):
+            select(slot, chunk * nchunk // 2, nchunk)
         for sub in range(nz):
             pair = chunk * nz + sub
             partner = dot(halfway[pair].reshape(nw * 2 * nb, 2 * W), sel_a[pair])
@@ -523,9 +544,12 @@
                     0,
                 ).astype(BF)
                 leading = jnp.where(lane < half, pltpu.roll(stacked, half, 1), stacked)
-            masked = jnp.where(same_q == 2 * (sub % pairs), leading, 0.0)
-            exchange = dot(trailing, masked.astype(BF))
-            totals.append(jnp.concatenate([t_re, t_im], 0) - exchange)
+                masked = jnp.concatenate(
+                    [jnp.where(same_q == 2 * i, leading, 0.0) for i in range(pairs)], 1
+                )
+                exchange = dot(trailing, masked.astype(BF))
+            at = sub % pairs * W
+            totals.append(jnp.concatenate([t_re, t_im], 0) - exchange[:, at : at + W])
         spot = shift_down(iota((2 * nb, W), 1), na) & (nz - 1)
         cols = pl.ds(pl.multiple_of(chunk * W, W), W)
         for z in range(nz):
@@ -553,6 +577,12 @@
     for dz in range(1, nz):
         for chunk in range(chunks):
             t_copy(dz, chunk).wait_send()
+
+
+def order_result(dense_ref, out_ref):
+    parts, na, nq, nb = out_ref.shape
+    for c in range(parts):
+        out_ref[c] = dense_ref[c * nb : (c + 1) * nb, :].T.reshape(na, nq, nb)
 
 
 def kernel_body(
@@ -597,7 +627,7 @@
             pltpu.VMEM((nz, 2 * nb, nq * na), BF),
             pltpu.VMEM((nz, 2 * nb, nq * na), BF),
             dma((6,)),
-            dma((CHUNKS,)),
+            dma((nv // PIECE + 1,)),
             dma((nw,)),
             dma((nw,)),
             dma((nw,)),
@@ -617,7 +647,13 @@
         cross_table,
         vertex_matrix[0],
     )
-    return out.reshape(2, nb, na, nq).transpose(0, 2, 3, 1)
+    return pl.pallas_call(
+        order_result,
+        out_shape=jax.ShapeDtypeStruct((2, na, nq, nb), F32),
+        in_specs=[vmem],
+        out_specs=vmem,
+        compiler_params=pltpu.CompilerParams(vmem_limit_bytes=VMEM_BYTES - 1024 * 1024),
+    )(out)
 
 
 def fits(mesh):
@@ -642,7 +678,7 @@
 
     def chosen(*args):
         matrix, plus = args[0], args[5]
-        small = fits(mesh) and PARTS * plus.shape[0] == W and matrix.shape[-1] % (128 * CHUNKS) == 0
+        small = fits(mesh) and PARTS * plus.shape[0] == W and matrix.shape[-1] % 128 == 0
         return (kernel_body if small else plain_body)(*args)
 
     return jax.shard_map(chosen, mesh=mesh, in_specs=in_specs, out_specs=out_specs, check_vma=False)

time: 28 us -> 28.7 us (1.025)
  Pallas kernels: 25.7 us -> 28.5 us
  local copies, waits for them, and re-layouts: 2.12 us -> 0 us
    reshape x2 -> x0, local copies, waits for them, and re-layouts: 2.12 us -> none  [kernel_body(): return out.reshape(2, nb, na, nq).transpose(0, 2, 3, 1)]
    pallas_call x0 -> x1, Pallas kernels: none -> 1.9 us  [kernel_body(): pl.pallas_call(order_result, out_shape=jax.ShapeDtypeStruct((2, na, nq, n...]
    pallas_call x1, Pallas kernels: 25.7 us -> 26.6 us  [kernel_body(): pl.pallas_call(functools.partial(kernel, nblk, ngroup), out_shape=jax.Sha...]
where the time goes in v5:
time: 28.7 us; the launch traced here: 28.5 us
  Pallas kernels  28.5 us (99%)
    pallas_call x1, Pallas kernels, kernel_body(): pl.pallas_call(functools.partial(kernel, nblk, ngroup), out_shape=jax.Sha...  26.6 us
    pallas_call x1, Pallas kernels, kernel_body(): pl.pallas_call(order_result, out_shape=jax.ShapeDtypeStruct((2, na, nq, n...  1.9 us

profile of v5, /device:TPU:0, one launch (start us, length us, event | category | flops | bytes accessed | tf_op | source)
XLA Modules:
  0.0 28.5 jit_solution(8935513613645954738)
XLA Ops:
  0.0 26.6 %shard_map.73.dense_ref = f32[64,512]{1,0:T(8,128)} custom-call(s32[1,1152]{1,0:T(1,128)} %site_hbm.1, s32[1,1152]{1,0:T(1,128)} %time_hbm.1, s32[1,1152]{1,0:T(1,128)} %spin_hbm.1, f32[2,128]{1,0:T(2,128)} %free_hbm.1, s32[32,128]{1,0:T(8,128)} %plus_hbm.1, s32[16,32]{1,0:T(8,128)} %cross_hbm.1, bf16[1152,1152]{1,0:T(8,128)(2,1)} %bitcast.1), custom_call_target="tpu_custom_call" | custom-call | tf_op jit(solution)/shard_map/pallas_call | solution.py:603
  26.6 1.9 %shard_map.74 = f32[2,16,32,32]{3,2,1,0:T(8,128)} custom-call(f32[64,512]{1,0:T(8,128)} %shard_map.73.dense_ref), custom_call_target="tpu_custom_call" | custom-call | tf_op jit(solution)/shard_map/pallas_call | solution.py:650

commit v6 on v5

--- a/solution.py
+++ b/solution.py
@@ -311,6 +311,51 @@
             rows[pl.ds(2 * W + at, 2 * NW), :] = c_both * down
             rows[pl.ds(3 * W + at, 2 * NW), :] = s_both * down
 
+    lane = iota((W, W), 1)
+    plus = plus_ref[...].astype(F32)
+    plus = jnp.concatenate([plus, jnp.zeros((W - nq, W), F32)], 0)
+    expand = one_hot(shift_down(lane, PARTS) == iota((W, W), 0))
+    index = dot(plus.T.astype(BF), expand).astype(jnp.int32)
+    plus = plus.astype(BF)
+    my_b = one_hot(iota((nb, W), 1) == iota((nb, W), 0) + nb * grp)
+    plus_b = dot_nt(my_b, plus).astype(jnp.int32)
+    place = shift_down(lane & (half - 1), na) * (na * INNER) + na * yy + (lane & (na - 1))
+    my_a = one_hot(iota((W, W), 0) == place)
+    prow[...] = dot(plus[:nq], my_a)
+    same = one_hot(iota((nq, nq), 0) == iota((nq, nq), 1))
+    cross = jnp.concatenate([cross_ref[...].astype(F32), jnp.zeros((W - na, nq), F32)], 0)
+    crossing = dot_nt(same, cross.astype(BF)).astype(jnp.int32)
+    crossing = (
+        shift_down(crossing, nchunk) * W
+        + (crossing & 1) * half
+        + (shift_down(crossing, 2) & (nz - 1)) * na
+        + iota((nq, W), 1)
+    )
+
+    def selectors(step):
+        share = nq // pieces
+        columns = pltpu.roll(plus_b, (W - step * share) % W, 1)
+        for i in range(share):
+            column = jnp.broadcast_to(columns[:, i : i + 1], (nb, W))
+            at = pl.multiple_of((step * share + i) * nb, nb)
+            sel_b[pl.ds(at, nb), :] = one_hot(column == iota((nb, W), 1))
+        low = lane < half
+        for i in range(share // 2):
+            pair = step * (share // 2) + i
+            first = prow[pl.ds(2 * pair, 1), :]
+            second = prow[pl.ds(2 * pair + 1, 1), :]
+            hit = iota((W, W), 0) == jnp.where(
+                low, jnp.broadcast_to(first, (W, W)), jnp.broadcast_to(second, (W, W))
+            ).astype(jnp.int32)
+            sel_a[pair, :W, :] = one_hot(hit & low)
+            sel_a[pair, W:, :] = one_hot(hit & (lane >= half))
+        share = na // pieces
+        columns = pltpu.roll(crossing, (W - step * share) % W, 1)
+        for i in range(share):
+            column = jnp.broadcast_to(columns[:, i : i + 1], (nq, nq * na))
+            at = pl.multiple_of((step * share + i) * nq, nq)
+            sel_out[pl.ds(at, nq), :] = one_hot(column == iota((nq, nq * na), 1))
+
     kern[...] = jnp.zeros_like(kern)
 
     def project(index, width):
@@ -325,6 +370,7 @@
 
     def project_piece(index, carry):
         project(index, PIECE)
+        selectors(index)
         return carry
 
     lax.fori_loop(0, pieces, project_piece, 0)
@@ -381,11 +427,6 @@
 
     greens = [g.astype(BF).astype(F32) for g in greens]
     turned = [g.astype(BF).astype(F32) for g in turned]
-    plus = plus_ref[...].astype(F32)
-    plus_turned = jnp.concatenate([plus, jnp.zeros((W - nq, W), F32)], 0).T
-    expand = one_hot(shift_down(iota((W, W), 1), PARTS) == iota((W, W), 0))
-    index = dot(plus_turned.astype(BF), expand).astype(jnp.int32)
-    lane = iota((W, W), 1)
     part = lane & (PARTS - 1)
 
     def choose(values):
@@ -414,47 +455,13 @@
     lr_copy(lr_for(near), near, near).start()
     lr[0] = lr_send[yy * nx + xx]
 
-    plus_bf = plus.astype(BF)
-    my_b = one_hot(iota((nb, W), 1) == iota((nb, W), 0) + nb * grp)
-    plus_b = dot_nt(my_b, plus_bf).astype(jnp.int32)
-    for q in range(nq):
-        column = jnp.broadcast_to(plus_b[:, q : q + 1], (nb, W))
-        sel_b[pl.ds(q * nb, nb), :] = one_hot(column == iota((nb, W), 1))
-    place = shift_down(lane & (half - 1), na) * (na * INNER) + na * yy + (lane & (na - 1))
-    my_a = one_hot(iota((W, W), 0) == place)
-    prow[...] = dot(plus_bf, my_a)
-
-    def pair_selector(pair, carry):
-        first = prow[pl.ds(2 * pair, 1), :]
-        second = prow[pl.ds(2 * pair + 1, 1), :]
-        low = lane < half
-        hit = iota((W, W), 0) == jnp.where(
-            low, jnp.broadcast_to(first, (W, W)), jnp.broadcast_to(second, (W, W))
-        ).astype(jnp.int32)
-        sel_a[pair, :W, :] = one_hot(hit & low)
-        sel_a[pair, W:, :] = one_hot(hit & (lane >= half))
-        return carry
-
-    lax.fori_loop(0, npair, pair_selector, 0)
-
-    same = one_hot(iota((nq, nq), 0) == iota((nq, nq), 1))
-    crossing = dot_nt(same, cross_ref[...].astype(F32).astype(BF)).astype(jnp.int32)
-    crossing = (
-        shift_down(crossing, nchunk) * W
-        + (crossing & 1) * half
-        + (shift_down(crossing, 2) & (nz - 1)) * na
-    )
-    for r in range(na):
-        column = jnp.broadcast_to(crossing[:, r : r + 1] + r, (nq, nq * na))
-        sel_out[pl.ds(r * nq, nq), :] = one_hot(column == iota((nq, nq * na), 1))
-
     def take_rows(slot):
         for c in range(2):
             mine = st[slot, pl.ds(pl.multiple_of(c * W + nb * grp, nb), nb), :]
             sb[slot, c] = dot(mine, my_a)
 
     def select(slot, pair, count):
-        picks = sel_b[pl.ds(pl.multiple_of(pair * 2 * nb, 2 * nb), count * nb), :]
+        picks = sel_b[pl.ds(pair * 2 * nb, count * nb), :]
         picked = dot_nt(picks, st[slot]).astype(BF)
         for q in range(count):
             for c in range(2):
@@ -464,8 +471,7 @@
 
     def first_selection(slot):
         take_rows(slot)
-        for chunk in range(nq // nchunk):
-            select(slot, chunk * nchunk // 2, nchunk)
+        select(slot, 0, nq)
 
     def own_chip(step, carry):
         @pl.when(step > 0)
@@ -483,7 +489,7 @@
 
     def forwarded(step, carry):
         st_copy(0, step, near).wait_recv()
-        take_rows(step)
+        first_selection(step)
         return carry
 
     lax.fori_loop(0, CORES, own_chip, 0)
@@ -515,8 +521,6 @@
 
     def measure_chunk(chunk, carry):
         totals = []
-        for slot in range(near + 1, CORES * near):
-            select(slot, chunk * nchunk // 2, nchunk)
         for sub in range(nz):
             pair = chunk * nz + sub
             partner = dot(halfway[pair].reshape(nw * 2 * nb, 2 * W), sel_a[pair])
@@ -678,7 +682,8 @@
 
     def chosen(*args):
         matrix, plus = args[0], args[5]
-        small = fits(mesh) and PARTS * plus.shape[0] == W and matrix.shape[-1] % 128 == 0
+        pieces = matrix.shape[-1] // PIECE
+        small = fits(mesh) and pieces and plus.shape[0] // 2 % pieces == 0 == W // mesh.shape["blk"] % pieces and PARTS * plus.shape[0] == W and matrix.shape[-1] % 128 == 0
         return (kernel_body if small else plain_body)(*args)
 
     return jax.shard_map(chosen, mesh=mesh, in_specs=in_specs, out_specs=out_specs, check_vma=False)

time: 28.7 us -> 29.2 us (1.017)
  Pallas kernels: 28.5 us -> 29 us
    pallas_call x1, Pallas kernels: 26.6 us -> 27.1 us  [kernel_body(): pl.pallas_call(functools.partial(kernel, nblk, ngroup), out_shape=jax.Sha...]
where the time goes in v6:
time: 29.2 us; the launch traced here: 29 us
  Pallas kernels  29 us (99%)
    pallas_call x1, Pallas kernels, kernel_body(): pl.pallas_call(functools.partial(kernel, nblk, ngroup), out_shape=jax.Sha...  27.1 us
    pallas_call x1, Pallas kernels, kernel_body(): pl.pallas_call(order_result, out_shape=jax.ShapeDtypeStruct((2, na, nq, n...  1.9 us

profile of v6, /device:TPU:0, one launch (start us, length us, event | category | flops | bytes accessed | tf_op | source)
XLA Modules:
  0.0 29.0 jit_solution(10376008415977067482)
XLA Ops:
  0.0 27.1 %shard_map.73.dense_ref = f32[64,512]{1,0:T(8,128)} custom-call(s32[1,1152]{1,0:T(1,128)} %site_hbm.1, s32[1,1152]{1,0:T(1,128)} %time_hbm.1, s32[1,1152]{1,0:T(1,128)} %spin_hbm.1, f32[2,128]{1,0:T(2,128)} %free_hbm.1, s32[32,128]{1,0:T(8,128)} %plus_hbm.1, s32[16,32]{1,0:T(8,128)} %cross_hbm.1, bf16[1152,1152]{1,0:T(8,128)(2,1)} %bitcast.1), custom_call_target="tpu_custom_call" | custom-call | tf_op jit(solution)/shard_map/pallas_call | solution.py:607
  27.1 1.9 %shard_map.74 = f32[2,16,32,32]{3,2,1,0:T(8,128)} custom-call(f32[64,512]{1,0:T(8,128)} %shard_map.73.dense_ref), custom_call_target="tpu_custom_call" | custom-call | tf_op jit(solution)/shard_map/pallas_call | solution.py:654

commit v7 on v4

--- a/solution.py
+++ b/solution.py
@@ -136,7 +136,6 @@
 CORES = 2
 VMEM_BYTES = 64 * 1024 * 1024
 PARTS = 4
-CHUNKS = 3
 
 
 def iota(shape, dim):
@@ -178,7 +177,6 @@
     cross_ref,
     matrix,
     rows,
-    kern,
     st,
     lr,
     lr_send,
@@ -214,6 +212,8 @@
     ]
     for copy in small:
         copy.start()
+    matrix_copy = pltpu.make_async_copy(matrix_hbm, matrix, matrix_sem)
+    matrix_copy.start()
 
     nz = nblk // INNER
     na = W // nblk
@@ -223,7 +223,6 @@
     npair = nq // 2
     nchunk = W // na
     nv = site_ref.shape[1]
-    piece = nv // CHUNKS
     blk = lax.axis_index("blk")
     grp = lax.axis_index("group")
     zz = blk // INNER
@@ -249,15 +248,6 @@
         pl.semaphore_signal(barrier, inc=1, device_id=plane_peer(slot), device_id_type=MESH)
     for dz in range(1, nz):
         pl.semaphore_signal(barrier, inc=1, device_id=z_peer(dz), device_id_type=MESH)
-
-    def matrix_copy(index):
-        cols = pl.ds(pl.multiple_of(index * piece, 128), piece)
-        return pltpu.make_async_copy(
-            matrix_hbm.at[:, cols], matrix.at[:, cols], matrix_sem.at[index]
-        )
-
-    for index in range(CHUNKS):
-        matrix_copy(index).start()
 
     for copy in small:
         copy.wait()
@@ -307,19 +297,12 @@
             rows[pl.ds(2 * W + at, 2 * NW), :] = c_both * down
             rows[pl.ds(3 * W + at, 2 * NW), :] = s_both * down
 
-    kern[...] = jnp.zeros_like(kern)
-
-    def project(index, carry):
-        matrix_copy(index).wait()
-        cols = pl.ds(pl.multiple_of(index * piece, 128), piece)
-        projected = dot(rows[...], matrix[:, cols]).astype(BF)
-        for s in range(2):
-            kern[s] += dot_nt(
-                projected[2 * W * s : 2 * W * (s + 1)], rows[pl.ds(2 * W * s, 2 * W), cols]
-            )
-        return carry
-
-    lax.fori_loop(0, CHUNKS, project, 0)
+    matrix_copy.wait()
+    projected = dot(rows[...], matrix[...]).astype(BF)
+    kern = [
+        dot_nt(projected[2 * W * s : 2 * W * (s + 1)], rows[2 * W * s : 2 * W * (s + 1), :])
+        for s in range(2)
+    ]
 
     ga_re = jnp.broadcast_to(free_ref[0:1, :], (W, W))
     ga_im = jnp.broadcast_to(free_ref[1:2, :], (W, W))
@@ -329,8 +312,8 @@
     norm_factor = 1.0 / math.sqrt(NV)
     greens = []
     for s in range(2):
-        k_re = kern[s, :W, :W] + kern[s, W:, W:]
-        k_im = kern[s, W:, :W] - kern[s, :W, W:]
+        k_re = kern[s][:W, :W] + kern[s][W:, W:]
+        k_im = kern[s][W:, :W] - kern[s][:W, W:]
         h_re = ga_re * k_re - ga_im * k_im
         h_im = ga_re * k_im + ga_im * k_re
         greens.append(-(h_re * gb_re - h_im * gb_im) * norm_factor)
@@ -459,6 +442,9 @@
     def same_core(step, carry):
         st_copy(0, step, near).wait_recv()
         st_copy(step, near + step, near).start()
+        return carry
+
+    def peers(step, carry):
         first_selection(step)
         return carry
 
@@ -469,6 +455,7 @@
 
     lax.fori_loop(0, CORES, own_chip, 0)
     lax.fori_loop(1, near, same_core, 0)
+    lax.fori_loop(1, near, peers, 0)
     for slot in range(1, near):
         lr_copy(lr.at[0], slot, near).wait_recv()
         lr_copy(lr.at[slot], near + slot, near).start()
@@ -555,6 +542,12 @@
             t_copy(dz, chunk).wait_send()
 
 
+def order_result(dense_ref, out_ref):
+    parts, na, nq, nb = out_ref.shape
+    for c in range(parts):
+        out_ref[c] = dense_ref[c * nb : (c + 1) * nb, :].T.reshape(na, nq, nb)
+
+
 def kernel_body(
     vertex_matrix, vertex_site, vertex_time, vertex_spin, free_green, plus_table, cross_table
 ):
@@ -584,7 +577,6 @@
             pltpu.VMEM(cross_table.shape, jnp.int32),
             pltpu.VMEM((nv, nv), BF),
             pltpu.VMEM((4 * W, nv), BF),
-            pltpu.VMEM((2, 2 * W, 2 * W), F32),
             pltpu.VMEM((nw, 2 * W, W), BF),
             pltpu.VMEM((nw, W, W), BF),
             pltpu.VMEM((nw // CORES, W, W), BF),
@@ -597,7 +589,7 @@
             pltpu.VMEM((nz, 2 * nb, nq * na), BF),
             pltpu.VMEM((nz, 2 * nb, nq * na), BF),
             dma((6,)),
-            dma((CHUNKS,)),
+            dma,
             dma((nw,)),
             dma((nw,)),
             dma((nw,)),
@@ -617,7 +609,13 @@
         cross_table,
         vertex_matrix[0],
     )
-    return out.reshape(2, nb, na, nq).transpose(0, 2, 3, 1)
+    return pl.pallas_call(
+        order_result,
+        out_shape=jax.ShapeDtypeStruct((2, na, nq, nb), F32),
+        in_specs=[vmem],
+        out_specs=vmem,
+        compiler_params=pltpu.CompilerParams(vmem_limit_bytes=VMEM_BYTES - 1024 * 1024),
+    )(out)
 
 
 def fits(mesh):
@@ -642,7 +640,7 @@
 
     def chosen(*args):
         matrix, plus = args[0], args[5]
-        small = fits(mesh) and PARTS * plus.shape[0] == W and matrix.shape[-1] % (128 * CHUNKS) == 0
+        small = fits(mesh) and PARTS * plus.shape[0] == W and matrix.shape[-1] % 128 == 0
         return (kernel_body if small else plain_body)(*args)
 
     return jax.shard_map(chosen, mesh=mesh, in_specs=in_specs, out_specs=out_specs, check_vma=False)

time: 28 us -> 27.7 us (0.989)
  local copies, waits for them, and re-layouts: 2.12 us -> 0 us
  Pallas kernels: 25.7 us -> 27.5 us
    reshape x2 -> x0, local copies, waits for them, and re-layouts: 2.12 us -> none  [kernel_body(): return out.reshape(2, nb, na, nq).transpose(0, 2, 3, 1)]
    pallas_call x0 -> x1, Pallas kernels: none -> 1.9 us  [kernel_body(): pl.pallas_call(order_result, out_shape=jax.ShapeDtypeStruct((2, na, nq, n...]
where the time goes in v7:
time: 27.7 us; the launch traced here: 27.5 us
  Pallas kernels  27.5 us (99%)
    pallas_call x1, Pallas kernels, kernel_body(): pl.pallas_call(functools.partial(kernel, nblk, ngroup), out_shape=jax.Sha...  25.6 us
    pallas_call x1, Pallas kernels, kernel_body(): pl.pallas_call(order_result, out_shape=jax.ShapeDtypeStruct((2, na, nq, n...  1.9 us

profile of v7, /device:TPU:0, one launch (start us, length us, event | category | flops | bytes accessed | tf_op | source)
XLA Modules:
  0.0 27.5 jit_solution(1727796671243724390)
XLA Ops:
  0.0 25.6 %shard_map.73.dense_ref = f32[64,512]{1,0:T(8,128)} custom-call(s32[1,1152]{1,0:T(1,128)} %site_hbm.1, s32[1,1152]{1,0:T(1,128)} %time_hbm.1, s32[1,1152]{1,0:T(1,128)} %spin_hbm.1, f32[2,128]{1,0:T(2,128)} %free_hbm.1, s32[32,128]{1,0:T(8,128)} %plus_hbm.1, s32[16,32]{1,0:T(8,128)} %cross_hbm.1, bf16[1152,1152]{1,0:T(8,128)(2,1)} %bitcast.1), custom_call_target="tpu_custom_call" | custom-call | tf_op jit(solution)/shard_map/pallas_call | solution.py:566
  25.6 1.9 %shard_map.74 = f32[2,16,32,32]{3,2,1,0:T(8,128)} custom-call(f32[64,512]{1,0:T(8,128)} %shard_map.73.dense_ref), custom_call_target="tpu_custom_call" | custom-call | tf_op jit(solution)/shard_map/pallas_call | solution.py:612

commit v8 on v7

--- a/solution.py
+++ b/solution.py
@@ -422,13 +422,13 @@
         sel_out[pl.ds(r * nq, nq), :] = one_hot(column == iota((nq, nq * na), 1))
 
     def first_selection(slot):
+        picked = dot_nt(sel_b[...], st[slot]).astype(BF)
         for c in range(2):
             mine = st[slot, pl.ds(pl.multiple_of(c * W + nb * grp, nb), nb), :]
             sb[slot, c] = dot(mine, my_a)
-            chosen = dot_nt(sel_b[...], st[slot, c * W : (c + 1) * W, :]).astype(BF)
             for q in range(nq):
-                halfway[q // 2, slot, c, :, pl.ds((q % 2) * W, W)] = chosen[
-                    q * nb : (q + 1) * nb
+                halfway[q // 2, slot, c, :, pl.ds((q % 2) * W, W)] = picked[
+                    q * nb : (q + 1) * nb, c * W : (c + 1) * W
                 ]
 
     def own_chip(step, carry):
@@ -510,9 +510,12 @@
                     0,
                 ).astype(BF)
                 leading = jnp.where(lane < half, pltpu.roll(stacked, half, 1), stacked)
-            masked = jnp.where(same_q == 2 * (sub % pairs), leading, 0.0)
-            exchange = dot(trailing, masked.astype(BF))
-            totals.append(jnp.concatenate([t_re, t_im], 0) - exchange)
+                masked = jnp.concatenate(
+                    [jnp.where(same_q == 2 * i, leading, 0.0) for i in range(pairs)], 1
+                )
+                exchange = dot(trailing, masked.astype(BF))
+            at = sub % pairs * W
+            totals.append(jnp.concatenate([t_re, t_im], 0) - exchange[:, at : at + W])
         spot = shift_down(iota((2 * nb, W), 1), na) & (nz - 1)
         cols = pl.ds(pl.multiple_of(chunk * W, W), W)
         for z in range(nz):

time: 27.7 us -> 27.6 us (level)
  no operation moved by 1% of the time
where the time goes in v8:
time: 27.6 us; the launch traced here: 27.5 us
  Pallas kernels  27.5 us (100%)
    pallas_call x1, Pallas kernels, kernel_body(): pl.pallas_call(functools.partial(kernel, nblk, ngroup), out_shape=jax.Sha...  25.6 us
    pallas_call x1, Pallas kernels, kernel_body(): pl.pallas_call(order_result, out_shape=jax.ShapeDtypeStruct((2, na, nq, n...  1.9 us

profile of v8, /device:TPU:0, one launch (start us, length us, event | category | flops | bytes accessed | tf_op | source)
XLA Modules:
  0.0 27.5 jit_solution(14309764483961844593)
XLA Ops:
  0.0 25.6 %shard_map.73.dense_ref = f32[64,512]{1,0:T(8,128)} custom-call(s32[1,1152]{1,0:T(1,128)} %site_hbm.1, s32[1,1152]{1,0:T(1,128)} %time_hbm.1, s32[1,1152]{1,0:T(1,128)} %spin_hbm.1, f32[2,128]{1,0:T(2,128)} %free_hbm.1, s32[32,128]{1,0:T(8,128)} %plus_hbm.1, s32[16,32]{1,0:T(8,128)} %cross_hbm.1, bf16[1152,1152]{1,0:T(8,128)(2,1)} %bitcast.1), custom_call_target="tpu_custom_call" | custom-call | tf_op jit(solution)/shard_map/pallas_call | solution.py:569
  25.6 1.9 %shard_map.74 = f32[2,16,32,32]{3,2,1,0:T(8,128)} custom-call(f32[64,512]{1,0:T(8,128)} %shard_map.73.dense_ref), custom_call_target="tpu_custom_call" | custom-call | tf_op jit(solution)/shard_map/pallas_call | solution.py:615

commit v9 on v8

--- a/solution.py
+++ b/solution.py
@@ -382,9 +382,8 @@
         for y in range(INNER):
             joined = jnp.where(lane < half, left, shifted(lead, half - half * y))
             lr_send[y * nx + x] = joined.astype(BF)
-    for slot in range(near - 1, 0, -1):
+    for slot in reversed(plane):
         lr_copy(lr_for(slot), slot, slot).start()
-    lr_copy(lr_for(near), near, near).start()
     lr[0] = lr_send[yy * nx + xx]
 
     plus_bf = plus.astype(BF)
@@ -456,12 +455,9 @@
     lax.fori_loop(0, CORES, own_chip, 0)
     lax.fori_loop(1, near, same_core, 0)
     lax.fori_loop(1, near, peers, 0)
-    for slot in range(1, near):
-        lr_copy(lr.at[0], slot, near).wait_recv()
-        lr_copy(lr.at[slot], near + slot, near).start()
     lax.fori_loop(near + 1, CORES * near, forwarded, 0)
 
-    for slot in range(near, CORES * near):
+    for slot in plane:
         lr_copy(lr.at[0], slot, near).wait_recv()
 
     nw = len(plane) + 1

time: 27.6 us -> 27.7 us (level)
  no operation moved by 1% of the time
where the time goes in v9:
time: 27.7 us; the launch traced here: 27.5 us
  Pallas kernels  27.5 us (99%)
    pallas_call x1, Pallas kernels, kernel_body(): pl.pallas_call(functools.partial(kernel, nblk, ngroup), out_shape=jax.Sha...  25.6 us
    pallas_call x1, Pallas kernels, kernel_body(): pl.pallas_call(order_result, out_shape=jax.ShapeDtypeStruct((2, na, nq, n...  1.9 us

profile of v9, /device:TPU:0, one launch (start us, length us, event | category | flops | bytes accessed | tf_op | source)
XLA Modules:
  0.0 27.5 jit_solution(9142923994867365885)
XLA Ops:
  0.0 25.6 %shard_map.73.dense_ref = f32[64,512]{1,0:T(8,128)} custom-call(s32[1,1152]{1,0:T(1,128)} %site_hbm.1, s32[1,1152]{1,0:T(1,128)} %time_hbm.1, s32[1,1152]{1,0:T(1,128)} %spin_hbm.1, f32[2,128]{1,0:T(2,128)} %free_hbm.1, s32[32,128]{1,0:T(8,128)} %plus_hbm.1, s32[16,32]{1,0:T(8,128)} %cross_hbm.1, bf16[1152,1152]{1,0:T(8,128)(2,1)} %bitcast.1), custom_call_target="tpu_custom_call" | custom-call | tf_op jit(solution)/shard_map/pallas_call | solution.py:565
  25.6 1.9 %shard_map.74 = f32[2,16,32,32]{3,2,1,0:T(8,128)} custom-call(f32[64,512]{1,0:T(8,128)} %shard_map.73.dense_ref), custom_call_target="tpu_custom_call" | custom-call | tf_op jit(solution)/shard_map/pallas_call | solution.py:611
